TPU v7x, 128 devices: a whole 4x4x4 slice. The times are simulated.
128 devices in a mesh: section: 8 (over z, core), dp: 16 (over y, x).
Axes of the slice: x: 4, y: 4, z: 4, core: 2. Of those that a mesh axis runs over, the one named last changes fastest.
Arguments:
- embedded: bfloat16 [2, 2048, 4096], P(None, 'dp'), may hold values from -6 to 6
- saved_inputs: bfloat16 [8, 2, 2048, 4096], P('section', None, 'dp'), may hold values from -6 to 6
- cotangent: bfloat16 [2, 2048, 4096], P(None, 'dp'), may hold values from -6 to 6
- w_down: bfloat16 [8, 512, 4096], P('section'), may hold values from -0.09375 to 0.09375
- w_up: bfloat16 [8, 512, 4096], P('section'), may hold values from -0.046875 to 0.046875
- bias: float32 [8, 4096], P('section'), may hold values from -3 to 3
- owners: int32 [2048, 2, 16, 1], P('dp'), may hold values from 0 to 127; in each aligned block of 512 rows (0 to 511, 512 to 1023, ..., all dimensions but the last counted through in order) at most 8 rows name the same one
- row_ids: int32 [2048, 2, 16], P('dp'), may hold values from 0 to 2047
Outputs:
- grad_down: float32 [8, 512, 4096], P('section', None, 'dp')
- grad_up: float32 [8, 512, 4096], P('section', None, 'dp')
- grad_bias: float32 [8, 4096], P('section', 'dp')
- table_grad: float32 [262144, 256], P(('section', 'dp'))
Inputs may be any that keep to these rules, and one draw needn't show every extreme that they name: `owners`: in each aligned block of 512 lookups in the order (sample, micro-batch, feature) no owner is named more than 8 times, a bound that some block reaches.
All inputs are finite; a program needn't handle non-finite values.
Results may differ from a plain program's by a relative error of at most 0.015.
Values may be sent and summed in bfloat16 or wider, within the bound.
No kernel may reach another device: no remote copies, remote signals or barrier semaphores. Data moves between devices by JAX's collectives and lax.ppermute only.
A program may use at most 192 MiB of HBM per device.

v0:
```python
import jax
import jax.numpy as jnp
from jax import lax
from jax.experimental.layout import Layout, with_layout_constraint
from jax.sharding import PartitionSpec as P

E = 256
ROWS_DEV = 2048
CAP = 8
BF = jnp.bfloat16
F32 = jnp.float32


def dot(a, b, dims):
    return lax.dot_general(a, b, (dims, ((), ())), preferred_element_type=F32)


def exchange(pieces, axis):
    return lax.all_to_all(pieces, axis, split_axis=0, concat_axis=0, tiled=True)


def rows_major(array):
    return with_layout_constraint(array, Layout(major_to_minor=tuple(range(array.ndim))))


def after(*arrays):
    return lax.optimization_barrier(arrays)


def in_columns(rows, devices):
    return rows.reshape(rows.shape[0], devices, -1).transpose(1, 0, 2)


def ring(sizes, place, shift):
    pairs = []
    stride = 1
    for size in sizes[place + 1 :]:
        stride *= size
    count = 1
    for size in sizes:
        count *= size
    for i in range(count):
        here = i // stride % sizes[place]
        pairs.append((i, i + ((here + shift) % sizes[place] - here) * stride))
    return pairs


def sum_over_section(terms, sections, section_id):
    chips = sections // 2
    chip, core = section_id // 2, section_id % 2
    pieces, rows, width = terms.shape
    terms = terms.reshape(pieces, chips, 2, rows // sections, width)
    other = lax.dynamic_index_in_dim(terms, 1 - core, 2, keepdims=False)
    mine = lax.dynamic_index_in_dim(terms, core, 2, keepdims=False)
    other = lax.ppermute(other, "section", ring((chips, 2), 1, 1))
    both = (mine.astype(F32) + other.astype(F32)).astype(BF)
    total = lax.dynamic_index_in_dim(both, chip, 1, keepdims=False).astype(F32)
    for d in range(1, chips):
        block = lax.dynamic_index_in_dim(both, (chip + d) % chips, 1, keepdims=False)
        total = total + lax.ppermute(block, "section", ring((chips, 2), 0, d)).astype(F32)
    return total.astype(BF).reshape(-1, width)


def local(embedded, saved_inputs, cotangent, w_down, w_up, bias, owners, row_ids):
    sections = lax.axis_size("section")
    replicas = lax.axis_size("dp")
    section_id = lax.axis_index("section")
    devices = sections * replicas
    pieces, rows, width = embedded.shape
    features = width // E
    rank = w_down.shape[1]
    share = rows // sections
    turns = sections + pieces - 1
    down, up = w_down[0], w_up[0]

    held_g, held_h = [None] * pieces, [None] * pieces
    odd = (sections - 1 - section_id) % 2 == 1
    incoming = jnp.zeros((rows, width), BF)
    layer_in = saved_inputs[0].reshape(-1, width)

    def piece_of(held, k):
        return jnp.where(odd, held[1 - k], held[k])

    def terms_of(k, passed):
        g = piece_of(held_g, k).astype(F32)
        bottom = jnp.where(section_id == 0, passed, jnp.zeros((), BF)).astype(F32)
        term = (g * product[k] + bottom).astype(BF)
        return term, in_columns((g * embedded[k].astype(F32)).astype(BF), replicas)

    last = []
    for turn in range(turns):
        piece = turn - (sections - 1 - section_id)
        valid = (piece >= 0) & (piece < pieces)
        clipped = jnp.clip(piece, 0, pieces - 1)
        first = lax.dynamic_index_in_dim(embedded, clipped, 0, keepdims=False)
        if turn == 2:
            incoming, latent = after(incoming, latent)
        if turn == 4:
            incoming, product = after(incoming, product)
        if turn == 6:
            incoming, all_in, put, ids = after(incoming, all_in, put, ids)
        if turn < pieces:
            incoming = jnp.where(section_id == sections - 1, cotangent[turn], incoming)
        gp = (incoming.astype(F32) * first.astype(F32)).astype(BF)
        h = dot(gp, up, ((1,), (1,))).astype(BF)
        passed = (incoming.astype(F32) + dot(h, down, ((1,), (0,)))).astype(BF)
        if turn < turns - 1:
            pairs = [(s, s - 1) for s in range(1, sections) if 0 <= turn - (sections - 1 - s) < pieces]
            arriving = lax.ppermute(passed, "section", pairs)
        slot = turn % pieces
        if turn < pieces:
            held_g[slot], held_h[slot] = incoming, h
        else:
            old_g, old_h, _ = after(held_g[slot], held_h[slot], passed)
            held_g[slot] = jnp.where(valid, incoming, old_g)
            held_h[slot] = jnp.where(valid, h, old_h)

        if turn == 1:
            there = rows_major(after(layer_in, passed)[0])
            latent = dot(there, down, ((1,), (1,))).astype(BF)
            all_in = rows_major(exchange(rows_major(in_columns(there, replicas)), "dp"))
        if turn == 3:
            latent, _ = after(latent, passed)
            product = (dot(latent, up, ((1,), (0,))) + bias[0]).reshape(pieces, rows, width)
            all_latent = lax.all_gather(latent, "dp", axis=0)
        if turn == 5:
            own, ids, _ = after(owners, row_ids, passed)
            own = lax.dynamic_slice_in_dim(own, section_id * share, share, 0).transpose(2, 1, 0, 3).reshape(-1)
            ids = lax.dynamic_slice_in_dim(ids, section_id * share, share, 0).transpose(2, 1, 0).reshape(-1)
            order = jnp.arange(own.shape[0], dtype=jnp.int32)
            earlier = (own[:, None] == own[None, :]) & (order[:, None] < order[None, :])
            place = own * CAP + jnp.sum(earlier.astype(jnp.int32), axis=0)
            put = jnp.arange(devices * CAP, dtype=jnp.int32)[:, None] == place[None, :]
            send_ids = jnp.sum(jnp.where(put, ids[None, :], 0), axis=1)
            put = put.astype(BF)
            ids = jnp.stack([send_ids // 256, send_ids % 256], axis=1).astype(BF)
            ids = rows_major(jnp.pad(ids, ((0, 0), (0, 126))))
        last.append(passed)
        if turn < turns - 1:
            incoming = arriving
    last = last[-pieces:]
    terms, columns = zip(*(terms_of(k, last[k]) for k in range(pieces)))
    all_h = lax.all_gather(jnp.stack([piece_of(held_h, k) for k in range(pieces)]), "dp", axis=0)
    summed = sum_over_section(jnp.stack(terms), sections, section_id)
    all_gp = exchange(jnp.concatenate(columns, axis=1), "dp")

    row_grads = in_columns(summed, features).reshape(-1, E)
    send = rows_major(dot(put, row_grads, ((1,), (0,))).astype(BF))
    send = jnp.concatenate([send, ids], axis=1).reshape(devices, CAP, -1)
    send, all_gp, all_latent = after(send, all_gp, all_latent)
    got = exchange(send, ("section", "dp")).reshape(devices * CAP, -1)
    got, all_h = after(got, all_h)
    got = rows_major(got)

    all_in = all_in.reshape(replicas, pieces, rows, -1)
    grad_down = dot(all_h, all_in, ((0, 1, 2), (0, 1, 2)))
    grad_up = dot(all_latent, all_gp, ((0, 1), (0, 1)))
    grad_bias = jnp.sum(all_gp.astype(F32), axis=(0, 1))

    got_ids = (got[:, E].astype(F32) * 256 + got[:, E + 1].astype(F32)).astype(jnp.int32)
    table_put = (jnp.arange(ROWS_DEV, dtype=jnp.int32)[:, None] == got_ids[None, :]).astype(BF)
    table_grad = dot(table_put, got[:, :E], ((1,), (0,)))
    return (grad_down[None], grad_up[None], grad_bias[None], table_grad)


def solution(mesh):
    placed = (
        P(None, "dp", None),
        P("section", None, "dp", None),
        P(None, "dp", None),
        P("section", None, None),
        P("section", None, None),
        P("section", None),
        P("dp", None, None, None),
        P("dp", None, None),
    )
    return jax.shard_map(
        local,
        mesh=mesh,
        in_specs=placed,
        out_specs=(
            P("section", None, "dp"),
            P("section", None, "dp"),
            P("section", "dp"),
            P(("section", "dp"), None),
        ),
        check_vma=False,
    )
```

profile of v0, /device:TPU:1, one launch (start us, length us, event | category | flops | bytes accessed | tf_op | source)
XLA Modules:
  0.0 231.3 jit_solution(8793039102477218076)
XLA Ops:
  9.1 4.5 %fusion.60 = bf16[128,512]{1,0:T(8,128)(2,1)S(1)} fusion(bf16[1,512,4096]{2,1,0:T(8,128)(2,1)} %param.12, bf16[2,128,4096]{2,1,0:T(8,128)(2,1)S(1)} %copy-done.10, s32[]{:T(128)S(6)} %min.28, bf16[2,128,4096]{2,1,0:T(8,128)(2,1)} %param.10, pred[]{:T(512)S(6)} %eq.58), kind=kOutput, calls=%fused_computation.94 | convolution fusion | flops 539557888 | bytes 6422533 | tf_op jit(solution)/shard_map/dot_general | solution.py:15
  17.6 3.9 %fusion.63 = bf16[128,512]{1,0:T(8,128)(2,1)S(1)} fusion(bf16[1,512,4096]{2,1,0:T(8,128)(2,1)} %param.12, bf16[128,4096]{1,0:T(8,128)(2,1)S(1)} %bitcast_select_fusion, bf16[2,128,4096]{2,1,0:T(8,128)(2,1)S(1)} %copy-done.10, s32[]{:T(128)S(6)} %min.29), kind=kOutput, calls=%fused_computation.95 | convolution fusion | flops 539033600 | bytes 6422532 | tf_op jit(solution)/shard_map/dot_general | solution.py:15
  24.9 4.1 %copy.67 = bf16[256,4096]{0,1:T(8,128)(2,1)} copy(bf16[256,4096]{1,0:T(8,128)(2,1)} %bitcast.221) | data formatting | bytes 4194304 | tf_op jit(solution)/shard_map/layout_constraint | solution.py:23
  28.9 3.9 %copy.68 = bf16[256,16,256]{2,0,1:T(8,128)(2,1)} copy(bf16[256,16,256]{0,2,1:T(8,128)(2,1)} %bitcast.214) | data formatting | bytes 4194304 | tf_op jit(solution)/shard_map/reshape | solution.py:31
  32.9 7.6 %all-to-all-start = ((bf16[16,256,256]{2,1,0:T(8,128)(2,1)}), bf16[16,256,256]{2,1,0:T(8,128)(2,1)}, u32[]{:S(2)}, u32[]{:S(2)}) async-start(bf16[16,256,256]{2,1,0:T(8,128)(2,1)} %bitcast.213), calls=%async_computation | async-start | bytes 4194304 | tf_op jit(solution)/shard_map/all_to_all | solution.py:19
  40.6 4.8 %fusion.57 = bf16[256,512]{1,0:T(8,128)(2,1)} fusion(bf16[256,4096]{1,0:T(8,128)(2,1)} %bitcast.222, bf16[1,512,4096]{2,1,0:T(8,128)(2,1)} %param.11), kind=kOutput, calls=%fused_computation.93 | convolution fusion | flops 1073872896 | bytes 6553600 | tf_op jit(solution)/shard_map/dot_general | solution.py:15
  45.4 4.2 %fusion.66 = bf16[128,512]{1,0:T(8,128)(2,1)S(1)} fusion(bf16[1,512,4096]{2,1,0:T(8,128)(2,1)} %param.12, bf16[128,4096]{1,0:T(8,128)(2,1)} %collective-permute-done.1, bf16[2,128,4096]{2,1,0:T(8,128)(2,1)S(1)} %copy-done.10, s32[]{:T(128)S(6)} %min.30), kind=kOutput, calls=%fused_computation.96 | convolution fusion | flops 539033600 | bytes 6422532 | tf_op jit(solution)/shard_map/dot_general | solution.py:15
  59.5 5.7 %convolution_add_fusion = f32[256,4096]{1,0:T(8,128)} fusion(bf16[256,512]{1,0:T(8,128)(2,1)S(1)} %copy-done.31, bf16[1,512,4096]{2,1,0:T(8,128)(2,1)} %param.12, f32[4096]{0:T(1024)} %bitcast.226), kind=kOutput, calls=%fused_computation.2 | convolution fusion | flops 1074790400 | bytes 8667136 | tf_op jit(solution)/shard_map/dot_general | solution.py:15
  67.0 2.9 %fusion.72 = bf16[128,512]{1,0:T(8,128)(2,1)S(1)} fusion(bf16[1,512,4096]{2,1,0:T(8,128)(2,1)S(1)} %copy-done.3, bf16[128,4096]{1,0:T(8,128)(2,1)} %collective-permute-done.3, bf16[2,128,4096]{2,1,0:T(8,128)(2,1)S(1)} %copy-done.10, s32[]{:T(128)S(6)} %min.32), kind=kOutput, calls=%fused_computation.98 | convolution fusion | flops 539033600 | bytes 6422532 | tf_op jit(solution)/shard_map/dot_general | solution.py:15
  83.3 22.4 %collective-permute-done.5 = bf16[128,4096]{1,0:T(8,128)(2,1)S(1)} collective-permute-done((bf16[128,4096]{1,0:T(8,128)(2,1)}, bf16[128,4096]{1,0:T(8,128)(2,1)S(1)}, u32[]{:S(2)}, u32[]{:S(2)}) %collective-permute-start.5) | collective-permute-done | bytes 1048608 | tf_op jit(solution)/shard_map/ppermute | solution.py:109
  105.7 4.1 %fusion.78 = bf16[128,512]{1,0:T(8,128)(2,1)S(1)} fusion(bf16[1,512,4096]{2,1,0:T(8,128)(2,1)} %param.12, bf16[128,4096]{1,0:T(8,128)(2,1)S(1)} %collective-permute-done.5, bf16[2,128,4096]{2,1,0:T(8,128)(2,1)S(1)} %copy-done.10, s32[]{:T(128)S(6)} %min.34), kind=kOutput, calls=%fused_computation.100 | convolution fusion | flops 539033600 | bytes 6422532 | tf_op jit(solution)/shard_map/dot_general | solution.py:15
  110.6 2.2 collective-permute-start.6
  114.0 13.6 %collective-permute-done.6 = bf16[128,4096]{1,0:T(8,128)(2,1)S(1)} collective-permute-done((bf16[128,4096]{1,0:T(8,128)(2,1)S(1)}, bf16[128,4096]{1,0:T(8,128)(2,1)S(1)}, u32[]{:S(2)}, u32[]{:S(2)}) %collective-permute-start.6) | collective-permute-done | bytes 1048608 | tf_op jit(solution)/shard_map/ppermute | solution.py:109
  137.5 3.3 %fusion.51 = (bf16[128,4096]{1,0:T(8,128)(2,1)}, bf16[128,4096]{1,0:T(8,128)(2,1)S(1)}, bf16[128,4096]{1,0:T(8,128)(2,1)S(1)}) fusion(bf16[2,128,4096]{2,1,0:T(8,128)(2,1)S(1)} %copy-done.10, pred[]{:T(512)S(6)} %eq.65, bf16[128,4096]{1,0:T(8,128)(2,1)} %copy-done.13, bf16[128,4096]{1,0:T(8,128)(2,1)} %broadcast_select_fusion.2, pred[]{:T(512)S(6)} %and.93, ...), kind=kLoop, calls=%fused_computation.79 | loop fusion | flops 3670016 | bytes 8388611 | tf_op jit(solution)/shard_map/convert_element_type | solution.py:88
  140.9 2.2 fusion.53
  147.7 6.9 %all-to-all-start.1 = ((bf16[16,256,256]{2,1,0:T(8,128)(2,1)}), bf16[16,256,256]{2,1,0:T(8,128)(2,1)S(1)}, u32[]{:S(2)}, u32[]{:S(2)}) async-start(bf16[16,256,256]{2,1,0:T(8,128)(2,1)} %pad_maximum_fusion), calls=%async_computation.1 | async-start | bytes 4194304 | tf_op jit(solution)/shard_map/all_to_all | solution.py:19
  159.4 7.6 %collective-permute-done.10 = bf16[2,16,4096]{2,1,0:T(8,128)(2,1)} collective-permute-done((bf16[2,16,4096]{2,1,0:T(8,128)(2,1)}, bf16[2,16,4096]{2,1,0:T(8,128)(2,1)}, u32[]{:S(2)}, u32[]{:S(2)}) %collective-permute-start.10) | collective-permute-done | bytes 262176 | tf_op jit(solution)/shard_map/ppermute | solution.py:60
  167.6 6.0 %collective-permute-done.9 = bf16[2,16,4096]{2,1,0:T(8,128)(2,1)} collective-permute-done((bf16[2,16,4096]{2,1,0:T(8,128)(2,1)S(1)}, bf16[2,16,4096]{2,1,0:T(8,128)(2,1)}, u32[]{:S(2)}, u32[]{:S(2)}) %collective-permute-start.9) | collective-permute-done | bytes 262176 | tf_op jit(solution)/shard_map/ppermute | solution.py:60
  176.5 12.4 %all-to-all-done.1 = bf16[16,256,256]{2,1,0:T(8,128)(2,1)S(1)} async-done(((bf16[16,256,256]{2,1,0:T(8,128)(2,1)}), bf16[16,256,256]{2,1,0:T(8,128)(2,1)S(1)}, u32[]{:S(2)}, u32[]{:S(2)}) %all-to-all-start.1) | async-done | bytes 2097184 | tf_op jit(solution)/shard_map/all_to_all | solution.py:19
  188.9 4.6 %all-to-all-start.2 = ((bf16[128,8,384]{2,1,0:T(8,128)(2,1)}), bf16[128,8,384]{2,1,0:T(8,128)(2,1)S(1)}, u32[]{:S(2)}, u32[]{:S(2)}) async-start(bf16[128,8,384]{2,1,0:T(8,128)(2,1)} %maximum_bitcast_fusion), calls=%async_computation.2 | async-start | bytes 1572864 | tf_op jit(solution)/shard_map/all_to_all | solution.py:19
  194.6 4.3 %convolution_bitcast_fusion = f32[1,512,256]{2,1,0:T(8,128)} fusion(bf16[16,256,512]{2,1,0:T(8,128)(2,1)} %bitcast.229, bf16[16,256,256]{2,1,0:T(8,128)(2,1)S(1)} %all-to-all-done.1), kind=kOutput, calls=%fused_computation.91 | convolution fusion | flops 1073741824 | bytes 6815744 | tf_op jit(solution)/shard_map/dot_general | solution.py:15
  198.9 18.6 %all-to-all-done.2 = bf16[128,8,384]{2,1,0:T(8,128)(2,1)S(1)} async-done(((bf16[128,8,384]{2,1,0:T(8,128)(2,1)}), bf16[128,8,384]{2,1,0:T(8,128)(2,1)S(1)}, u32[]{:S(2)}, u32[]{:S(2)}) %all-to-all-start.2) | async-done | bytes 786464 | tf_op jit(solution)/shard_map/all_to_all | solution.py:19
  217.8 2.9 %fusion = f32[2048,256]{1,0:T(8,128)} fusion(s32[1024]{0:T(1024)S(1)} %convert_reduce_fusion.2, bf16[1024,384]{1,0:T(8,128)(2,1)S(1)} %bitcast.220), kind=kOutput, calls=%fused_computation.1 | convolution fusion | flops 1075838976 | bytes 2625536 | tf_op jit(solution)/shard_map/dot_general | solution.py:15
  220.7 3.7 %convolution_bitcast_fusion.1 = f32[1,512,256]{2,1,0:T(8,128)} fusion(bf16[16,2,128,512]{3,2,1,0:T(8,128)(2,1)S(1)} %bitcast.212, bf16[16,2,128,256]{3,2,1,0:T(8,128)(2,1)} %bitcast.43), kind=kOutput, calls=%fused_computation.92 | convolution fusion | flops 1073741824 | bytes 6815744 | tf_op jit(solution)/shard_map/dot_general | solution.py:15
  (161 shorter events, 60.1 us)
Async XLA Ops:
  7.2 72.0 %copy-start = (s32[128,2,16,1]{0,3,2,1:T(1,128)S(1)}, s32[128,2,16,1]{0,3,2,1:T(1,128)}, u32[]{:S(2)}) copy-start(s32[128,2,16,1]{0,3,2,1:T(1,128)} %param.14) | copy-start | bytes 49156
  14.3 1.7 collective-permute-start
  23.2 22.1 %collective-permute-start.1 = (bf16[128,4096]{1,0:T(8,128)(2,1)}, bf16[128,4096]{1,0:T(8,128)(2,1)}, u32[]{:S(2)}, u32[]{:S(2)}) collective-permute-start(bf16[128,4096]{1,0:T(8,128)(2,1)} %fusion.2), channel_id=1, source_target_pairs={{96,80},{112,96},{97,81},{113,97},{98,82},{114,98},{99,83},{115,99... | collective-permute-start | bytes 3145736 | tf_op jit(solution)/shard_map/ppermute | solution.py:109
  32.9 50.4 %all-to-all-start = ((bf16[16,256,256]{2,1,0:T(8,128)(2,1)}), bf16[16,256,256]{2,1,0:T(8,128)(2,1)}, u32[]{:S(2)}, u32[]{:S(2)}) async-start(bf16[16,256,256]{2,1,0:T(8,128)(2,1)} %bitcast.213), calls=%async_computation | async-start | bytes 4194304 | tf_op jit(solution)/shard_map/all_to_all | solution.py:19
  40.5 148.4 %all-gather.5.cloned.1.call-start = ((), (), s32[]{:S(2)}) async-start(), calls=%async_computation.3 | async-start | bytes 4456448 | tf_op jit(solution)/shard_map/all_gather | solution.py:125
  51.7 2.5 %collective-permute-start.2 = (bf16[128,4096]{1,0:T(8,128)(2,1)S(1)}, bf16[128,4096]{1,0:T(8,128)(2,1)S(1)}, u32[]{:S(2)}, u32[]{:S(2)}) collective-permute-start(bf16[128,4096]{1,0:T(8,128)(2,1)S(1)} %fusion.3), channel_id=1, source_target_pairs={{80,64},{96,80},{81,65},{97,81},{82,66},{98,82},{83,67},{99,83},{8... | collective-permute-start | bytes 3145736 | tf_op jit(solution)/shard_map/ppermute | solution.py:109
  57.5 9.5 %collective-permute-start.3 = (bf16[128,4096]{1,0:T(8,128)(2,1)}, bf16[128,4096]{1,0:T(8,128)(2,1)}, u32[]{:S(2)}, u32[]{:S(2)}) collective-permute-start(bf16[128,4096]{1,0:T(8,128)(2,1)} %fusion.4), channel_id=1, source_target_pairs={{64,48},{80,64},{65,49},{81,65},{66,50},{82,66},{67,51},{83,67},{6... | collective-permute-start | bytes 3145736 | tf_op jit(solution)/shard_map/ppermute | solution.py:109
  59.2 158.3 %all-gather.7.cloned.1.call-start = ((), (), s32[]{:S(2)}) async-start(), calls=%async_computation.4 | async-start | bytes 4456448 | tf_op jit(solution)/shard_map/all_gather | solution.py:143
  59.4 6.4 %copy-start.19 = (bf16[128,4096]{1,0:T(8,128)(2,1)S(1)}, bf16[128,4096]{1,0:T(8,128)(2,1)}, u32[]{:S(2)}) copy-start(bf16[128,4096]{1,0:T(8,128)(2,1)} %copy-done.18) | copy-start | bytes 3145732
  59.4 7.5 %copy-start.3 = (bf16[1,512,4096]{2,1,0:T(8,128)(2,1)S(1)}, bf16[1,512,4096]{2,1,0:T(8,128)(2,1)}, u32[]{:S(2)}) copy-start(bf16[1,512,4096]{2,1,0:T(8,128)(2,1)} %param.12) | copy-start | bytes 12582916
  72.0 2.7 %collective-permute-start.4 = (bf16[128,4096]{1,0:T(8,128)(2,1)S(1)}, bf16[128,4096]{1,0:T(8,128)(2,1)S(1)}, u32[]{:S(2)}, u32[]{:S(2)}) collective-permute-start(bf16[128,4096]{1,0:T(8,128)(2,1)S(1)} %fusion.5), channel_id=1, source_target_pairs={{48,32},{64,48},{49,33},{65,49},{50,34},{66,50},{51,35},{67,51},{5... | collective-permute-start | bytes 3145736 | tf_op jit(solution)/shard_map/ppermute | solution.py:109
  77.9 27.8 %collective-permute-start.5 = (bf16[128,4096]{1,0:T(8,128)(2,1)}, bf16[128,4096]{1,0:T(8,128)(2,1)S(1)}, u32[]{:S(2)}, u32[]{:S(2)}) collective-permute-start(bf16[128,4096]{1,0:T(8,128)(2,1)} %fusion.6), channel_id=1, source_target_pairs={{32,16},{48,32},{33,17},{49,33},{34,18},{50,34},{35,19},{51,35},{3... | collective-permute-start | bytes 3145736 | tf_op jit(solution)/shard_map/ppermute | solution.py:109
  83.3 26.6 %copy-start.9 = (bf16[1,512,4096]{2,1,0:T(8,128)(2,1)S(1)}, bf16[1,512,4096]{2,1,0:T(8,128)(2,1)}, u32[]{:S(2)}) copy-start(bf16[1,512,4096]{2,1,0:T(8,128)(2,1)} %param.11) | copy-start | bytes 12582916
  109.9 17.7 %copy-start.4 = (bf16[1,512,4096]{2,1,0:T(8,128)(2,1)S(1)}, bf16[1,512,4096]{2,1,0:T(8,128)(2,1)}, u32[]{:S(2)}) copy-start(bf16[1,512,4096]{2,1,0:T(8,128)(2,1)} %param.12) | copy-start | bytes 12582916
  110.6 17.0 %collective-permute-start.6 = (bf16[128,4096]{1,0:T(8,128)(2,1)S(1)}, bf16[128,4096]{1,0:T(8,128)(2,1)S(1)}, u32[]{:S(2)}, u32[]{:S(2)}) collective-permute-start(bf16[128,4096]{1,0:T(8,128)(2,1)S(1)} %fusion.7), channel_id=1, source_target_pairs={{16,0},{32,16},{17,1},{33,17},{18,2},{34,18},{19,3},{35,19},{20,4}... | collective-permute-start | bytes 3145736 | tf_op jit(solution)/shard_map/ppermute | solution.py:109
  129.9 3.6 %collective-permute-start.7 = (bf16[128,4096]{1,0:T(8,128)(2,1)S(1)}, bf16[128,4096]{1,0:T(8,128)(2,1)S(1)}, u32[]{:S(2)}, u32[]{:S(2)}) collective-permute-start(bf16[128,4096]{1,0:T(8,128)(2,1)S(1)} %fusion.8), channel_id=1, source_target_pairs={{16,0},{17,1},{18,2},{19,3},{20,4},{21,5},{22,6},{23,7},{24,8},{25... | collective-permute-start | bytes 3145736 | tf_op jit(solution)/shard_map/ppermute | solution.py:109
  144.3 10.3 %collective-permute-start.8 = (bf16[2,4,16,4096]{3,2,0,1:T(8,128)(2,1)}, bf16[2,4,16,4096]{3,2,0,1:T(8,128)(2,1)}, u32[]{:S(2)}, u32[]{:S(2)}) collective-permute-start(bf16[2,4,16,4096]{3,2,0,1:T(8,128)(2,1)} %bitcast.210), channel_id=1, source_target_pairs={{0,16},{16,0},{32,48},{48,32},{64,80},{80,64},{96,112},{112,96},{1... | collective-permute-start | bytes 3145736 | tf_op jit(solution)/shard_map/ppermute | solution.py:55
  147.7 41.1 %all-to-all-start.1 = ((bf16[16,256,256]{2,1,0:T(8,128)(2,1)}), bf16[16,256,256]{2,1,0:T(8,128)(2,1)S(1)}, u32[]{:S(2)}, u32[]{:S(2)}) async-start(bf16[16,256,256]{2,1,0:T(8,128)(2,1)} %pad_maximum_fusion), calls=%async_computation.1 | async-start | bytes 4194304 | tf_op jit(solution)/shard_map/all_to_all | solution.py:19
  157.1 18.0 %copy-start.26 = (bf16[1024,512]{1,0:T(8,128)(2,1)S(1)}, bf16[1024,512]{1,0:T(8,128)(2,1)}, u32[]{:S(2)}) copy-start(bf16[1024,512]{1,0:T(8,128)(2,1)} %fusion.56) | copy-start | bytes 3145732
  157.9 9.1 %collective-permute-start.10 = (bf16[2,16,4096]{2,1,0:T(8,128)(2,1)}, bf16[2,16,4096]{2,1,0:T(8,128)(2,1)}, u32[]{:S(2)}, u32[]{:S(2)}) collective-permute-start(bf16[2,16,4096]{2,1,0:T(8,128)(2,1)} %get-tuple-element.78), channel_id=1, source_target_pairs={{0,64},{16,80},{32,96},{48,112},{64,0},{80,16},{96,32},{112,48},{1... | collective-permute-start | bytes 786440 | tf_op jit(solution)/shard_map/ppermute | solution.py:60
  157.9 9.6 %collective-permute-start.11 = (bf16[2,16,4096]{2,1,0:T(8,128)(2,1)}, bf16[2,16,4096]{2,1,0:T(8,128)(2,1)}, u32[]{:S(2)}, u32[]{:S(2)}) collective-permute-start(bf16[2,16,4096]{2,1,0:T(8,128)(2,1)} %get-tuple-element.77), channel_id=1, source_target_pairs={{0,96},{16,112},{32,0},{48,16},{64,32},{80,48},{96,64},{112,80},{1... | collective-permute-start | bytes 786440 | tf_op jit(solution)/shard_map/ppermute | solution.py:60
  158.1 15.5 %collective-permute-start.9 = (bf16[2,16,4096]{2,1,0:T(8,128)(2,1)S(1)}, bf16[2,16,4096]{2,1,0:T(8,128)(2,1)}, u32[]{:S(2)}, u32[]{:S(2)}) collective-permute-start(bf16[2,16,4096]{2,1,0:T(8,128)(2,1)S(1)} %get-tuple-element.76), channel_id=1, source_target_pairs={{0,32},{16,48},{32,64},{48,80},{64,96},{80,112},{96,0},{112,16},{1... | collective-permute-start | bytes 786440 | tf_op jit(solution)/shard_map/ppermute | solution.py:60
  159.4 16.1 %copy-start.34 = (bf16[1024,128]{1,0:T(8,128)(2,1)S(1)}, bf16[1024,128]{1,0:T(8,128)(2,1)}, u32[]{:S(2)}) copy-start(bf16[1024,128]{1,0:T(8,128)(2,1)} %pad.4) | copy-start | bytes 786436
  188.9 28.7 %all-to-all-start.2 = ((bf16[128,8,384]{2,1,0:T(8,128)(2,1)}), bf16[128,8,384]{2,1,0:T(8,128)(2,1)S(1)}, u32[]{:S(2)}, u32[]{:S(2)}) async-start(bf16[128,8,384]{2,1,0:T(8,128)(2,1)} %maximum_bitcast_fusion), calls=%async_computation.2 | async-start | bytes 1572864 | tf_op jit(solution)/shard_map/all_to_all | solution.py:19
  (33 other events, 96.7 us)
Sparse Core Ops, SparseCore 0:
  59.3 70.6 all-gather.4
  137.6 77.2 all-gather.6
where the time goes:
time: 232 us; the launch traced here: 231 us
  waiting for transfers between devices  82.1 us (35%)
  matrix products  60.5 us (26%)
  starting transfers between devices  32.8 us (14%)
  other arithmetic  26.5 us (11%)
  between operations  14.8 us (6%)
  local copies, waits for them, and re-layouts  14.5 us (6%)
    dot_general x24, matrix products, dot(): return lax.dot_general(a, b, (dims, ((), ())), preferred_element_type=F32)  60.5 us
    ppermute x8, waiting for transfers between devices, local(): arriving = lax.ppermute(passed, 'section', pairs)  36.9 us
    all_to_all x3, waiting for transfers between devices, exchange(): return lax.all_to_all(pieces, axis, split_axis=0, concat_axis=0, tiled=True)  31 us
    all_to_all x3, starting transfers between devices, exchange(): return lax.all_to_all(pieces, axis, split_axis=0, concat_axis=0, tiled=True)  19.1 us
    ppermute x3, waiting for transfers between devices, sum_over_section(): lax.ppermute(block, 'section', ring((chips, 2), 0, d)).astype(F32)  14.2 us
    ppermute x8, starting transfers between devices, local(): arriving = lax.ppermute(passed, 'section', pairs)  11.6 us
    select_n x5, other arithmetic, local(): held_g[slot] = jnp.where(valid, incoming, old_g)  5.65 us
  transfers between devices with their start and end apart: 17, of which 8 were waited for; matrix products, arithmetic and copies ran while one was open for 34% of the time, Pallas kernels for 0%

commit v1 on v0

--- a/solution.py
+++ b/solution.py
@@ -45,7 +45,7 @@
     return pairs
 
 
-def sum_over_section(terms, sections, section_id):
+def sum_over_section(terms, sections, section_id, later):
     chips = sections // 2
     chip, core = section_id // 2, section_id % 2
     pieces, rows, width = terms.shape
@@ -54,11 +54,12 @@
     mine = lax.dynamic_index_in_dim(terms, core, 2, keepdims=False)
     other = lax.ppermute(other, "section", ring((chips, 2), 1, 1))
     both = (mine.astype(F32) + other.astype(F32)).astype(BF)
+    both, later = after(both, later)
     total = lax.dynamic_index_in_dim(both, chip, 1, keepdims=False).astype(F32)
     for d in range(1, chips):
         block = lax.dynamic_index_in_dim(both, (chip + d) % chips, 1, keepdims=False)
         total = total + lax.ppermute(block, "section", ring((chips, 2), 0, d)).astype(F32)
-    return total.astype(BF).reshape(-1, width)
+    return total.astype(BF).reshape(-1, width), later
 
 
 def local(embedded, saved_inputs, cotangent, w_down, w_up, bias, owners, row_ids):
@@ -75,7 +76,6 @@
 
     held_g, held_h = [None] * pieces, [None] * pieces
     odd = (sections - 1 - section_id) % 2 == 1
-    incoming = jnp.zeros((rows, width), BF)
     layer_in = saved_inputs[0].reshape(-1, width)
 
     def piece_of(held, k):
@@ -87,7 +87,6 @@
         term = (g * product[k] + bottom).astype(BF)
         return term, in_columns((g * embedded[k].astype(F32)).astype(BF), replicas)
 
-    last = []
     for turn in range(turns):
         piece = turn - (sections - 1 - section_id)
         valid = (piece >= 0) & (piece < pieces)
@@ -99,7 +98,9 @@
             incoming, product = after(incoming, product)
         if turn == 6:
             incoming, all_in, put, ids = after(incoming, all_in, put, ids)
-        if turn < pieces:
+        if turn == 0:
+            incoming = cotangent[0]
+        elif turn < pieces:
             incoming = jnp.where(section_id == sections - 1, cotangent[turn], incoming)
         gp = (incoming.astype(F32) * first.astype(F32)).astype(BF)
         h = dot(gp, up, ((1,), (1,))).astype(BF)
@@ -135,27 +136,31 @@
             put = put.astype(BF)
             ids = jnp.stack([send_ids // 256, send_ids % 256], axis=1).astype(BF)
             ids = rows_major(jnp.pad(ids, ((0, 0), (0, 126))))
-        last.append(passed)
+        if turn == sections - 1:
+            early = terms_of(0, passed)
+            arriving, *early = after(arriving, *early)
         if turn < turns - 1:
             incoming = arriving
-    last = last[-pieces:]
-    terms, columns = zip(*(terms_of(k, last[k]) for k in range(pieces)))
+    terms, columns = zip(early, terms_of(1, passed))
     all_h = lax.all_gather(jnp.stack([piece_of(held_h, k) for k in range(pieces)]), "dp", axis=0)
-    summed = sum_over_section(jnp.stack(terms), sections, section_id)
-    all_gp = exchange(jnp.concatenate(columns, axis=1), "dp")
+    columns = list(columns)
+    summed, columns[0] = sum_over_section(jnp.stack(terms), sections, section_id, columns[0])
+    all_gp = [exchange(columns[0], "dp")]
 
     row_grads = in_columns(summed, features).reshape(-1, E)
     send = rows_major(dot(put, row_grads, ((1,), (0,))).astype(BF))
     send = jnp.concatenate([send, ids], axis=1).reshape(devices, CAP, -1)
-    send, all_gp, all_latent = after(send, all_gp, all_latent)
+    send, all_gp[0], all_latent = after(send, all_gp[0], all_latent)
     got = exchange(send, ("section", "dp")).reshape(devices * CAP, -1)
-    got, all_h = after(got, all_h)
     got = rows_major(got)
+    columns[1], got, all_h = after(columns[1], got, all_h)
+    all_gp.append(exchange(columns[1], "dp"))
 
     all_in = all_in.reshape(replicas, pieces, rows, -1)
     grad_down = dot(all_h, all_in, ((0, 1, 2), (0, 1, 2)))
-    grad_up = dot(all_latent, all_gp, ((0, 1), (0, 1)))
-    grad_bias = jnp.sum(all_gp.astype(F32), axis=(0, 1))
+    all_latent = all_latent.reshape(replicas, pieces, rows, -1)
+    grad_up = sum(dot(all_latent[:, k], all_gp[k], ((0, 1), (0, 1))) for k in range(pieces))
+    grad_bias = sum(jnp.sum(gp.astype(F32), axis=(0, 1)) for gp in all_gp)
 
     got_ids = (got[:, E].astype(F32) * 256 + got[:, E + 1].astype(F32)).astype(jnp.int32)
     table_put = (jnp.arange(ROWS_DEV, dtype=jnp.int32)[:, None] == got_ids[None, :]).astype(BF)

time: 232 us -> 236 us (1.017)
  waiting for transfers between devices: 82.1 us -> 75.1 us
  starting transfers between devices: 32.8 us -> 39.6 us
    ppermute x3, waiting for transfers between devices: 14.2 us -> 6.95 us  [sum_over_section(): lax.ppermute(block, 'section', ring((chips, 2), 0, d)).astype(F32)]
    all_to_all x3 -> x4, starting transfers between devices: 19.1 us -> 26.1 us  [exchange(): return lax.all_to_all(pieces, axis, split_axis=0, concat_axis=0, tiled=True)]
    convert_element_type x1 -> x2, other arithmetic: 2.19 us -> 5.69 us  [terms_of(): term = (g * product[k] + bottom).astype(BF)]
    ppermute x1, waiting for transfers between devices: 0.01 us -> 3 us  [sum_over_section(): other = lax.ppermute(other, 'section', ring((chips, 2), 1, 1))]
    all_to_all x3 -> x4, waiting for transfers between devices: 31 us -> 28.4 us  [exchange(): return lax.all_to_all(pieces, axis, split_axis=0, concat_axis=0, tiled=True)]
    reshape x1 -> x3, local copies, waits for them, and re-layouts: 3.92 us -> 6.07 us  [in_columns(): return rows.reshape(rows.shape[0], devices, -1).transpose(1, 0, 2)]
    dot_general x24 -> x25, matrix products: 60.5 us -> 62.6 us  [dot(): return lax.dot_general(a, b, (dims, ((), ())), preferred_element_type=F32)]
    select_n x5 -> x4, other arithmetic: 5.65 us -> 3.62 us  [local(): held_g[slot] = jnp.where(valid, incoming, old_g)]
  transfers between devices with their start and end apart: 17 -> 18, of which waited for: 8 -> 9; matrix products, arithmetic and copies ran while one was open for 34% -> 37% of each run, Pallas kernels for 0% -> 0%
where the time goes in v1:
time: 236 us; the launch traced here: 234 us
  waiting for transfers between devices  75.1 us (32%)
  matrix products  62.6 us (27%)
  starting transfers between devices  39.6 us (17%)
  other arithmetic  25.6 us (11%)
  local copies, waits for them, and re-layouts  16.4 us (7%)
  between operations  14.8 us (6%)
    dot_general x25, matrix products, dot(): return lax.dot_general(a, b, (dims, ((), ())), preferred_element_type=F32)  62.6 us
    ppermute x8, waiting for transfers between devices, local(): arriving = lax.ppermute(passed, 'section', pairs)  36.7 us
    all_to_all x4, waiting for transfers between devices, exchange(): return lax.all_to_all(pieces, axis, split_axis=0, concat_axis=0, tiled=True)  28.4 us
    all_to_all x4, starting transfers between devices, exchange(): return lax.all_to_all(pieces, axis, split_axis=0, concat_axis=0, tiled=True)  26.1 us
    ppermute x8, starting transfers between devices, local(): arriving = lax.ppermute(passed, 'section', pairs)  11.6 us
    ppermute x3, waiting for transfers between devices, sum_over_section(): lax.ppermute(block, 'section', ring((chips, 2), 0, d)).astype(F32)  6.95 us
    reshape x3, local copies, waits for them, and re-layouts, in_columns(): return rows.reshape(rows.shape[0], devices, -1).transpose(1, 0, 2)  6.07 us
    convert_element_type x2, other arithmetic, terms_of(): term = (g * product[k] + bottom).astype(BF)  5.69 us
  transfers between devices with their start and end apart: 18, of which 9 were waited for; matrix products, arithmetic and copies ran while one was open for 37% of the time, Pallas kernels for 0%

profile of v1, /device:TPU:1, one launch (start us, length us, event | category | flops | bytes accessed | tf_op | source)
XLA Modules:
  0.0 234.0 jit_solution(16332930906074144948)
XLA Ops:
  7.2 4.5 %fusion.66 = bf16[128,512]{1,0:T(8,128)(2,1)S(1)} fusion(bf16[1,512,4096]{2,1,0:T(8,128)(2,1)} %param.12, bf16[2,128,4096]{2,1,0:T(8,128)(2,1)} %param.8, s32[]{:T(128)S(6)} %min.28, bf16[2,128,4096]{2,1,0:T(8,128)(2,1)} %param.10), kind=kOutput, calls=%fused_computation.101 | convolution fusion | flops 539033600 | bytes 6422532 | tf_op jit(solution)/shard_map/dot_general | solution.py:15
  16.1 3.9 %fusion.69 = bf16[128,512]{1,0:T(8,128)(2,1)S(1)} fusion(bf16[1,512,4096]{2,1,0:T(8,128)(2,1)} %param.12, bf16[128,4096]{1,0:T(8,128)(2,1)S(1)} %bitcast_select_fusion, bf16[2,128,4096]{2,1,0:T(8,128)(2,1)S(1)} %copy-done.10, s32[]{:T(128)S(6)} %min.29), kind=kOutput, calls=%fused_computation.102 | convolution fusion | flops 539033600 | bytes 6422532 | tf_op jit(solution)/shard_map/dot_general | solution.py:15
  24.5 4.1 %copy.70 = bf16[256,4096]{0,1:T(8,128)(2,1)} copy(bf16[256,4096]{1,0:T(8,128)(2,1)} %bitcast.251) | data formatting | bytes 4194304 | tf_op jit(solution)/shard_map/layout_constraint | solution.py:23
  28.5 3.9 %copy.71 = bf16[256,16,256]{2,0,1:T(8,128)(2,1)} copy(bf16[256,16,256]{0,2,1:T(8,128)(2,1)} %bitcast.245) | data formatting | bytes 4194304 | tf_op jit(solution)/shard_map/reshape | solution.py:31
  32.4 7.6 %all-to-all-start = ((bf16[16,256,256]{2,1,0:T(8,128)(2,1)}), bf16[16,256,256]{2,1,0:T(8,128)(2,1)}, u32[]{:S(2)}, u32[]{:S(2)}) async-start(bf16[16,256,256]{2,1,0:T(8,128)(2,1)} %bitcast.244), calls=%async_computation | async-start | bytes 4194304 | tf_op jit(solution)/shard_map/all_to_all | solution.py:19
  40.1 4.8 %fusion.63 = bf16[256,512]{1,0:T(8,128)(2,1)} fusion(bf16[256,4096]{1,0:T(8,128)(2,1)} %bitcast.252, bf16[1,512,4096]{2,1,0:T(8,128)(2,1)} %param.11), kind=kOutput, calls=%fused_computation.100 | convolution fusion | flops 1073872896 | bytes 6553600 | tf_op jit(solution)/shard_map/dot_general | solution.py:15
  44.9 4.2 %fusion.72 = bf16[128,512]{1,0:T(8,128)(2,1)S(1)} fusion(bf16[1,512,4096]{2,1,0:T(8,128)(2,1)} %param.12, bf16[128,4096]{1,0:T(8,128)(2,1)} %collective-permute-done.1, bf16[2,128,4096]{2,1,0:T(8,128)(2,1)S(1)} %copy-done.10, s32[]{:T(128)S(6)} %min.30), kind=kOutput, calls=%fused_computation.103 | convolution fusion | flops 539033600 | bytes 6422532 | tf_op jit(solution)/shard_map/dot_general | solution.py:15
  59.1 5.7 %convolution_add_fusion = f32[256,4096]{1,0:T(8,128)} fusion(bf16[256,512]{1,0:T(8,128)(2,1)S(1)} %copy-done.31, bf16[1,512,4096]{2,1,0:T(8,128)(2,1)} %param.12, f32[4096]{0:T(1024)} %bitcast.256), kind=kOutput, calls=%fused_computation.2 | convolution fusion | flops 1074790400 | bytes 8667136 | tf_op jit(solution)/shard_map/dot_general | solution.py:15
  66.6 2.9 %fusion.78 = bf16[128,512]{1,0:T(8,128)(2,1)S(1)} fusion(bf16[1,512,4096]{2,1,0:T(8,128)(2,1)S(1)} %copy-done.3, bf16[128,4096]{1,0:T(8,128)(2,1)} %collective-permute-done.3, bf16[2,128,4096]{2,1,0:T(8,128)(2,1)S(1)} %copy-done.10, s32[]{:T(128)S(6)} %min.32), kind=kOutput, calls=%fused_computation.105 | convolution fusion | flops 539033600 | bytes 6422532 | tf_op jit(solution)/shard_map/dot_general | solution.py:15
  83.0 22.2 %collective-permute-done.5 = bf16[128,4096]{1,0:T(8,128)(2,1)S(1)} collective-permute-done((bf16[128,4096]{1,0:T(8,128)(2,1)}, bf16[128,4096]{1,0:T(8,128)(2,1)S(1)}, u32[]{:S(2)}, u32[]{:S(2)}) %collective-permute-start.5) | collective-permute-done | bytes 1048608 | tf_op jit(solution)/shard_map/ppermute | solution.py:110
  105.2 4.1 %fusion.84 = bf16[128,512]{1,0:T(8,128)(2,1)S(1)} fusion(bf16[1,512,4096]{2,1,0:T(8,128)(2,1)} %param.12, bf16[128,4096]{1,0:T(8,128)(2,1)S(1)} %collective-permute-done.5, bf16[2,128,4096]{2,1,0:T(8,128)(2,1)S(1)} %copy-done.10, s32[]{:T(128)S(6)} %min.34), kind=kOutput, calls=%fused_computation.107 | convolution fusion | flops 539033600 | bytes 6422532 | tf_op jit(solution)/shard_map/dot_general | solution.py:15
  112.4 14.5 %collective-permute-done.6 = bf16[128,4096]{1,0:T(8,128)(2,1)S(1)} collective-permute-done((bf16[128,4096]{1,0:T(8,128)(2,1)S(1)}, bf16[128,4096]{1,0:T(8,128)(2,1)S(1)}, u32[]{:S(2)}, u32[]{:S(2)}) %collective-permute-start.6) | collective-permute-done | bytes 1048608 | tf_op jit(solution)/shard_map/ppermute | solution.py:110
  138.9 4.1 %fusion.54 = (bf16[128,4096]{1,0:T(8,128)(2,1)S(1)}, bf16[128,4096]{1,0:T(8,128)(2,1)}) fusion(f32[2,128,4096]{2,1,0:T(8,128)} %bitcast.241, bf16[128,4096]{1,0:T(8,128)(2,1)} %fusion.9, pred[]{:T(512)S(6)} %eq.65, bf16[128,4096]{1,0:T(8,128)(2,1)} %copy-done.20, bf16[128,4096]{1,0:T(8,128)(2,1)S(1)} %collective-permute-done.7, ...), kind=kLoop, calls=%fused_computation.81 | loop fusion | flops 4194304 | bytes 8388611 | tf_op jit(solution)/shard_map/convert_element_type | solution.py:87
  144.2 3.0 %collective-permute-done.8 = bf16[2,4,16,4096]{3,2,0,1:T(8,128)(2,1)} collective-permute-done((bf16[2,4,16,4096]{3,2,0,1:T(8,128)(2,1)}, bf16[2,4,16,4096]{3,2,0,1:T(8,128)(2,1)}, u32[]{:S(2)}, u32[]{:S(2)}) %collective-permute-start.8) | collective-permute-done | bytes 1048608 | tf_op jit(solution)/shard_map/ppermute | solution.py:55
  151.4 6.9 %all-to-all-start.1 = ((bf16[16,128,256]{2,1,0:T(8,128)(2,1)}), bf16[16,128,256]{2,1,0:T(8,128)(2,1)}, u32[]{:S(2)}, u32[]{:S(2)}) async-start(bf16[16,128,256]{2,1,0:T(8,128)(2,1)} %bitcast.249), calls=%async_computation.1 | async-start | bytes 2097152 | tf_op jit(solution)/shard_map/all_to_all | solution.py:19
  160.2 5.1 %collective-permute-done.9 = bf16[2,16,4096]{2,1,0:T(8,128)(2,1)} collective-permute-done((bf16[2,16,4096]{2,1,0:T(8,128)(2,1)S(1)}, bf16[2,16,4096]{2,1,0:T(8,128)(2,1)}, u32[]{:S(2)}, u32[]{:S(2)}) %collective-permute-start.9) | collective-permute-done | bytes 262176 | tf_op jit(solution)/shard_map/ppermute | solution.py:61
  168.1 6.3 %all-to-all-done.1 = bf16[16,128,256]{2,1,0:T(8,128)(2,1)} async-done(((bf16[16,128,256]{2,1,0:T(8,128)(2,1)}), bf16[16,128,256]{2,1,0:T(8,128)(2,1)}, u32[]{:S(2)}, u32[]{:S(2)}) %all-to-all-start.1) | async-done | bytes 1048608 | tf_op jit(solution)/shard_map/all_to_all | solution.py:19
  174.3 7.7 %all-to-all-start.2 = ((bf16[128,8,384]{2,1,0:T(8,128)(2,1)}), bf16[128,8,384]{2,1,0:T(8,128)(2,1)}, u32[]{:S(2)}, u32[]{:S(2)}) async-start(bf16[128,8,384]{2,1,0:T(8,128)(2,1)} %maximum_bitcast_fusion), calls=%async_computation.2 | async-start | bytes 1572864 | tf_op jit(solution)/shard_map/all_to_all | solution.py:19
  186.6 17.1 %all-to-all-done.2 = bf16[128,8,384]{2,1,0:T(8,128)(2,1)} async-done(((bf16[128,8,384]{2,1,0:T(8,128)(2,1)}), bf16[128,8,384]{2,1,0:T(8,128)(2,1)}, u32[]{:S(2)}, u32[]{:S(2)}) %all-to-all-start.2) | async-done | bytes 786464 | tf_op jit(solution)/shard_map/all_to_all | solution.py:19
  203.7 3.9 %all-to-all-start.3 = ((bf16[16,128,256]{2,1,0:T(8,128)(2,1)}), bf16[16,128,256]{2,1,0:T(8,128)(2,1)S(1)}, u32[]{:S(2)}, u32[]{:S(2)}) async-start(bf16[16,128,256]{2,1,0:T(8,128)(2,1)} %bitcast.237), calls=%async_computation.3 | async-start | bytes 2097152 | tf_op jit(solution)/shard_map/all_to_all | solution.py:19
  210.4 4.1 %fusion = f32[2048,256]{1,0:T(8,128)} fusion(s32[1024]{0:T(1024)S(1)} %convert_reduce_fusion.3, bf16[1024,384]{1,0:T(8,128)(2,1)} %bitcast.39), kind=kOutput, calls=%fused_computation.1 | convolution fusion | flops 1075838976 | bytes 2625536 | tf_op jit(solution)/shard_map/dot_general | solution.py:15
  214.6 3.7 %convolution_bitcast_fusion = f32[1,512,256]{2,1,0:T(8,128)} fusion(bf16[16,2,128,512]{3,2,1,0:T(8,128)(2,1)S(1)} %bitcast.243, bf16[16,2,128,256]{3,2,1,0:T(8,128)(2,1)} %bitcast.43), kind=kOutput, calls=%fused_computation.97 | convolution fusion | flops 1073741824 | bytes 6815744 | tf_op jit(solution)/shard_map/dot_general | solution.py:15
  218.2 5.0 %all-to-all-done.3 = bf16[16,128,256]{2,1,0:T(8,128)(2,1)S(1)} async-done(((bf16[16,128,256]{2,1,0:T(8,128)(2,1)}), bf16[16,128,256]{2,1,0:T(8,128)(2,1)S(1)}, u32[]{:S(2)}, u32[]{:S(2)}) %all-to-all-start.3) | async-done | bytes 1048608 | tf_op jit(solution)/shard_map/all_to_all | solution.py:19
  224.0 3.1 %fusion.62 = f32[1,512,256]{2,1,0:T(8,128)} fusion(f32[512,256]{1,0:T(8,128)S(1)} %fusion.59, bf16[16,128,256]{2,1,0:T(8,128)(2,1)S(1)} %all-to-all-done.3, bf16[16,2,128,512]{3,2,1,0:T(8,128)(2,1)} %bitcast.259), kind=kOutput, calls=%fused_computation.99 | convolution fusion | flops 537001984 | bytes 4194304 | tf_op jit(solution)/shard_map/dot_general | solution.py:15
  (165 shorter events, 66.9 us)
Async XLA Ops:
  7.2 71.6 %copy-start = (s32[128,2,16,1]{0,3,2,1:T(1,128)S(1)}, s32[128,2,16,1]{0,3,2,1:T(1,128)}, u32[]{:S(2)}) copy-start(s32[128,2,16,1]{0,3,2,1:T(1,128)} %param.14) | copy-start | bytes 49156
  12.6 1.8 collective-permute-start
  21.8 23.2 %collective-permute-start.1 = (bf16[128,4096]{1,0:T(8,128)(2,1)}, bf16[128,4096]{1,0:T(8,128)(2,1)}, u32[]{:S(2)}, u32[]{:S(2)}) collective-permute-start(bf16[128,4096]{1,0:T(8,128)(2,1)} %fusion.2), channel_id=1, source_target_pairs={{96,80},{112,96},{97,81},{113,97},{98,82},{114,98},{99,83},{115,99... | collective-permute-start | bytes 3145736 | tf_op jit(solution)/shard_map/ppermute | solution.py:110
  32.4 50.6 %all-to-all-start = ((bf16[16,256,256]{2,1,0:T(8,128)(2,1)}), bf16[16,256,256]{2,1,0:T(8,128)(2,1)}, u32[]{:S(2)}, u32[]{:S(2)}) async-start(bf16[16,256,256]{2,1,0:T(8,128)(2,1)} %bitcast.244), calls=%async_computation | async-start | bytes 4194304 | tf_op jit(solution)/shard_map/all_to_all | solution.py:19
  40.1 134.3 %all-gather.5.cloned.1.call-start = ((), (), s32[]{:S(2)}) async-start(), calls=%async_computation.4 | async-start | bytes 4456448 | tf_op jit(solution)/shard_map/all_gather | solution.py:126
  51.3 2.6 %collective-permute-start.2 = (bf16[128,4096]{1,0:T(8,128)(2,1)S(1)}, bf16[128,4096]{1,0:T(8,128)(2,1)S(1)}, u32[]{:S(2)}, u32[]{:S(2)}) collective-permute-start(bf16[128,4096]{1,0:T(8,128)(2,1)S(1)} %fusion.3), channel_id=1, source_target_pairs={{80,64},{96,80},{81,65},{97,81},{82,66},{98,82},{83,67},{99,83},{8... | collective-permute-start | bytes 3145736 | tf_op jit(solution)/shard_map/ppermute | solution.py:110
  57.2 9.4 %collective-permute-start.3 = (bf16[128,4096]{1,0:T(8,128)(2,1)}, bf16[128,4096]{1,0:T(8,128)(2,1)}, u32[]{:S(2)}, u32[]{:S(2)}) collective-permute-start(bf16[128,4096]{1,0:T(8,128)(2,1)} %fusion.4), channel_id=1, source_target_pairs={{64,48},{80,64},{65,49},{81,65},{66,50},{82,66},{67,51},{83,67},{6... | collective-permute-start | bytes 3145736 | tf_op jit(solution)/shard_map/ppermute | solution.py:110
  58.8 144.8 %all-gather.7.cloned.1.call-start = ((), (), s32[]{:S(2)}) async-start(), calls=%async_computation.5 | async-start | bytes 4456448 | tf_op jit(solution)/shard_map/all_gather | solution.py:145
  71.6 2.6 %collective-permute-start.4 = (bf16[128,4096]{1,0:T(8,128)(2,1)S(1)}, bf16[128,4096]{1,0:T(8,128)(2,1)S(1)}, u32[]{:S(2)}, u32[]{:S(2)}) collective-permute-start(bf16[128,4096]{1,0:T(8,128)(2,1)S(1)} %fusion.5), channel_id=1, source_target_pairs={{48,32},{64,48},{49,33},{65,49},{50,34},{66,50},{51,35},{67,51},{5... | collective-permute-start | bytes 3145736 | tf_op jit(solution)/shard_map/ppermute | solution.py:110
  77.5 27.7 %collective-permute-start.5 = (bf16[128,4096]{1,0:T(8,128)(2,1)}, bf16[128,4096]{1,0:T(8,128)(2,1)S(1)}, u32[]{:S(2)}, u32[]{:S(2)}) collective-permute-start(bf16[128,4096]{1,0:T(8,128)(2,1)} %fusion.6), channel_id=1, source_target_pairs={{32,16},{48,32},{33,17},{49,33},{34,18},{50,34},{35,19},{51,35},{3... | collective-permute-start | bytes 3145736 | tf_op jit(solution)/shard_map/ppermute | solution.py:110
  83.0 26.3 %copy-start.9 = (bf16[1,512,4096]{2,1,0:T(8,128)(2,1)S(1)}, bf16[1,512,4096]{2,1,0:T(8,128)(2,1)}, u32[]{:S(2)}) copy-start(bf16[1,512,4096]{2,1,0:T(8,128)(2,1)} %param.11) | copy-start | bytes 12582916
  109.3 17.7 %copy-start.4 = (bf16[1,512,4096]{2,1,0:T(8,128)(2,1)S(1)}, bf16[1,512,4096]{2,1,0:T(8,128)(2,1)}, u32[]{:S(2)}) copy-start(bf16[1,512,4096]{2,1,0:T(8,128)(2,1)} %param.12) | copy-start | bytes 12582916
  110.1 16.9 %collective-permute-start.6 = (bf16[128,4096]{1,0:T(8,128)(2,1)S(1)}, bf16[128,4096]{1,0:T(8,128)(2,1)S(1)}, u32[]{:S(2)}, u32[]{:S(2)}) collective-permute-start(bf16[128,4096]{1,0:T(8,128)(2,1)S(1)} %fusion.7), channel_id=1, source_target_pairs={{16,0},{32,16},{17,1},{33,17},{18,2},{34,18},{19,3},{35,19},{20,4}... | collective-permute-start | bytes 3145736 | tf_op jit(solution)/shard_map/ppermute | solution.py:110
  129.3 5.5 %collective-permute-start.7 = (bf16[128,4096]{1,0:T(8,128)(2,1)S(1)}, bf16[128,4096]{1,0:T(8,128)(2,1)S(1)}, u32[]{:S(2)}, u32[]{:S(2)}) collective-permute-start(bf16[128,4096]{1,0:T(8,128)(2,1)S(1)} %fusion.8), channel_id=1, source_target_pairs={{16,0},{17,1},{18,2},{19,3},{20,4},{21,5},{22,6},{23,7},{24,8},{25... | collective-permute-start | bytes 3145736 | tf_op jit(solution)/shard_map/ppermute | solution.py:110
  144.2 3.0 %collective-permute-start.8 = (bf16[2,4,16,4096]{3,2,0,1:T(8,128)(2,1)}, bf16[2,4,16,4096]{3,2,0,1:T(8,128)(2,1)}, u32[]{:S(2)}, u32[]{:S(2)}) collective-permute-start(bf16[2,4,16,4096]{3,2,0,1:T(8,128)(2,1)} %bitcast.240), channel_id=1, source_target_pairs={{0,16},{16,0},{32,48},{48,32},{64,80},{80,64},{96,112},{112,96},{1... | collective-permute-start | bytes 3145736 | tf_op jit(solution)/shard_map/ppermute | solution.py:55
  149.8 9.4 %collective-permute-start.10 = (bf16[2,16,4096]{2,1,0:T(8,128)(2,1)S(1)}, bf16[2,16,4096]{2,1,0:T(8,128)(2,1)S(1)}, u32[]{:S(2)}, u32[]{:S(2)}) collective-permute-start(bf16[2,16,4096]{2,1,0:T(8,128)(2,1)S(1)} %get-tuple-element.89), channel_id=1, source_target_pairs={{0,64},{16,80},{32,96},{48,112},{64,0},{80,16},{96,32},{112,48},{1... | collective-permute-start | bytes 786440 | tf_op jit(solution)/shard_map/ppermute | solution.py:61
  149.9 10.3 %collective-permute-start.11 = (bf16[2,16,4096]{2,1,0:T(8,128)(2,1)S(1)}, bf16[2,16,4096]{2,1,0:T(8,128)(2,1)S(1)}, u32[]{:S(2)}, u32[]{:S(2)}) collective-permute-start(bf16[2,16,4096]{2,1,0:T(8,128)(2,1)S(1)} %get-tuple-element.88), channel_id=1, source_target_pairs={{0,96},{16,112},{32,0},{48,16},{64,32},{80,48},{96,64},{112,80},{1... | collective-permute-start | bytes 786440 | tf_op jit(solution)/shard_map/ppermute | solution.py:61
  150.5 14.8 %collective-permute-start.9 = (bf16[2,16,4096]{2,1,0:T(8,128)(2,1)S(1)}, bf16[2,16,4096]{2,1,0:T(8,128)(2,1)}, u32[]{:S(2)}, u32[]{:S(2)}) collective-permute-start(bf16[2,16,4096]{2,1,0:T(8,128)(2,1)S(1)} %get-tuple-element.87), channel_id=1, source_target_pairs={{0,32},{16,48},{32,64},{48,80},{64,96},{80,112},{96,0},{112,16},{1... | collective-permute-start | bytes 786440 | tf_op jit(solution)/shard_map/ppermute | solution.py:61
  151.4 22.9 %all-to-all-start.1 = ((bf16[16,128,256]{2,1,0:T(8,128)(2,1)}), bf16[16,128,256]{2,1,0:T(8,128)(2,1)}, u32[]{:S(2)}, u32[]{:S(2)}) async-start(bf16[16,128,256]{2,1,0:T(8,128)(2,1)} %bitcast.249), calls=%async_computation.1 | async-start | bytes 2097152 | tf_op jit(solution)/shard_map/all_to_all | solution.py:19
  158.3 8.3 %copy-start.26 = (bf16[1024,512]{1,0:T(8,128)(2,1)S(1)}, bf16[1024,512]{1,0:T(8,128)(2,1)}, u32[]{:S(2)}) copy-start(bf16[1024,512]{1,0:T(8,128)(2,1)} %fusion.58) | copy-start | bytes 3145732
  158.3 8.7 %copy-start.34 = (bf16[1024,128]{1,0:T(8,128)(2,1)S(1)}, bf16[1024,128]{1,0:T(8,128)(2,1)}, u32[]{:S(2)}) copy-start(bf16[1024,128]{1,0:T(8,128)(2,1)} %pad.4) | copy-start | bytes 786436
  166.6 15.4 %copy-start.23 = (bf16[128,4096]{1,0:T(8,128)(2,1)S(1)}, bf16[128,4096]{1,0:T(8,128)(2,1)}, u32[]{:S(2)}) copy-start(bf16[128,4096]{1,0:T(8,128)(2,1)} %get-tuple-element.79) | copy-start | bytes 3145732
  174.3 29.3 %all-to-all-start.2 = ((bf16[128,8,384]{2,1,0:T(8,128)(2,1)}), bf16[128,8,384]{2,1,0:T(8,128)(2,1)}, u32[]{:S(2)}, u32[]{:S(2)}) async-start(bf16[128,8,384]{2,1,0:T(8,128)(2,1)} %maximum_bitcast_fusion), calls=%async_computation.2 | async-start | bytes 1572864 | tf_op jit(solution)/shard_map/all_to_all | solution.py:19
  203.7 19.5 %all-to-all-start.3 = ((bf16[16,128,256]{2,1,0:T(8,128)(2,1)}), bf16[16,128,256]{2,1,0:T(8,128)(2,1)S(1)}, u32[]{:S(2)}, u32[]{:S(2)}) async-start(bf16[16,128,256]{2,1,0:T(8,128)(2,1)} %bitcast.237), calls=%async_computation.3 | async-start | bytes 2097152 | tf_op jit(solution)/shard_map/all_to_all | solution.py:19
  (33 other events, 113.2 us)
Sparse Core Ops, SparseCore 0:
  59.0 70.4 all-gather.4
  138.9 60.7 all-gather.6

commit v2 on v0

--- a/solution.py
+++ b/solution.py
@@ -75,7 +75,6 @@
 
     held_g, held_h = [None] * pieces, [None] * pieces
     odd = (sections - 1 - section_id) % 2 == 1
-    incoming = jnp.zeros((rows, width), BF)
     layer_in = saved_inputs[0].reshape(-1, width)
 
     def piece_of(held, k):
@@ -87,7 +86,6 @@
         term = (g * product[k] + bottom).astype(BF)
         return term, in_columns((g * embedded[k].astype(F32)).astype(BF), replicas)
 
-    last = []
     for turn in range(turns):
         piece = turn - (sections - 1 - section_id)
         valid = (piece >= 0) & (piece < pieces)
@@ -99,7 +97,9 @@
             incoming, product = after(incoming, product)
         if turn == 6:
             incoming, all_in, put, ids = after(incoming, all_in, put, ids)
-        if turn < pieces:
+        if turn == 0:
+            incoming = cotangent[0]
+        elif turn < pieces:
             incoming = jnp.where(section_id == sections - 1, cotangent[turn], incoming)
         gp = (incoming.astype(F32) * first.astype(F32)).astype(BF)
         h = dot(gp, up, ((1,), (1,))).astype(BF)
@@ -135,11 +135,12 @@
             put = put.astype(BF)
             ids = jnp.stack([send_ids // 256, send_ids % 256], axis=1).astype(BF)
             ids = rows_major(jnp.pad(ids, ((0, 0), (0, 126))))
-        last.append(passed)
+        if turn == sections - 1:
+            early = terms_of(0, passed)
+            arriving, *early = after(arriving, *early)
         if turn < turns - 1:
             incoming = arriving
-    last = last[-pieces:]
-    terms, columns = zip(*(terms_of(k, last[k]) for k in range(pieces)))
+    terms, columns = zip(early, terms_of(1, passed))
     all_h = lax.all_gather(jnp.stack([piece_of(held_h, k) for k in range(pieces)]), "dp", axis=0)
     summed = sum_over_section(jnp.stack(terms), sections, section_id)
     all_gp = exchange(jnp.concatenate(columns, axis=1), "dp")
@@ -149,13 +150,13 @@
     send = jnp.concatenate([send, ids], axis=1).reshape(devices, CAP, -1)
     send, all_gp, all_latent = after(send, all_gp, all_latent)
     got = exchange(send, ("section", "dp")).reshape(devices * CAP, -1)
-    got, all_h = after(got, all_h)
-    got = rows_major(got)
 
     all_in = all_in.reshape(replicas, pieces, rows, -1)
+    grad_up = dot(all_latent.reshape(replicas, -1, rank), all_gp, ((0, 1), (0, 1)))
+    grad_bias = jnp.sum(all_gp.astype(F32), axis=(0, 1))
     grad_down = dot(all_h, all_in, ((0, 1, 2), (0, 1, 2)))
-    grad_up = dot(all_latent, all_gp, ((0, 1), (0, 1)))
-    grad_bias = jnp.sum(all_gp.astype(F32), axis=(0, 1))
+    got, grad_down = after(got, grad_down)
+    got = rows_major(got)
 
     got_ids = (got[:, E].astype(F32) * 256 + got[:, E + 1].astype(F32)).astype(jnp.int32)
     table_put = (jnp.arange(ROWS_DEV, dtype=jnp.int32)[:, None] == got_ids[None, :]).astype(BF)

time: 232 us -> 230 us (level)
  waiting for transfers between devices: 82.1 us -> 78.1 us
  local copies, waits for them, and re-layouts: 14.5 us -> 17.6 us
    all_to_all x3, waiting for transfers between devices: 31 us -> 12.1 us  [exchange(): return lax.all_to_all(pieces, axis, split_axis=0, concat_axis=0, tiled=True)]
    all_gather x1, waiting for transfers between devices: 0.01 us -> 15.1 us  [local(): lax.all_gather(jnp.stack([piece_of(held_h, k) for k in range(pieces)]), '...]
    reshape x1 -> x3, local copies, waits for them, and re-layouts: 3.92 us -> 6.31 us  [in_columns(): return rows.reshape(rows.shape[0], devices, -1).transpose(1, 0, 2)]
    select_n x5 -> x4, other arithmetic: 5.65 us -> 3.61 us  [local(): held_g[slot] = jnp.where(valid, incoming, old_g)]
  transfers between devices with their start and end apart: 17 -> 17, of which waited for: 8 -> 7; matrix products, arithmetic and copies ran while one was open for 34% -> 37% of each run, Pallas kernels for 0% -> 0%
where the time goes in v2:
time: 230 us
  waiting for transfers between devices  78.1 us (34%)
  matrix products  61.5 us (27%)
  starting transfers between devices  33.2 us (14%)
  other arithmetic  24.3 us (11%)
  local copies, waits for them, and re-layouts  17.6 us (8%)
  between operations  14.8 us (6%)
    dot_general x24, matrix products, dot(): return lax.dot_general(a, b, (dims, ((), ())), preferred_element_type=F32)  61.5 us
    ppermute x8, waiting for transfers between devices, local(): arriving = lax.ppermute(passed, 'section', pairs)  36.7 us
    all_to_all x3, starting transfers between devices, exchange(): return lax.all_to_all(pieces, axis, split_axis=0, concat_axis=0, tiled=True)  19.9 us
    all_gather x1, waiting for transfers between devices, local(): lax.all_gather(jnp.stack([piece_of(held_h, k) for k in range(pieces)]), '...  15.1 us
    ppermute x3, waiting for transfers between devices, sum_over_section(): lax.ppermute(block, 'section', ring((chips, 2), 0, d)).astype(F32)  14.2 us
    all_to_all x3, waiting for transfers between devices, exchange(): return lax.all_to_all(pieces, axis, split_axis=0, concat_axis=0, tiled=True)  12.1 us
    ppermute x8, starting transfers between devices, local(): arriving = lax.ppermute(passed, 'section', pairs)  11.6 us
    reshape x3, local copies, waits for them, and re-layouts, in_columns(): return rows.reshape(rows.shape[0], devices, -1).transpose(1, 0, 2)  6.31 us
  transfers between devices with their start and end apart: 17, of which 7 were waited for; matrix products, arithmetic and copies ran while one was open for 37% of the time, Pallas kernels for 0%

profile of v2, /device:TPU:1, one launch (start us, length us, event | category | flops | bytes accessed | tf_op | source)
XLA Modules:
  0.0 229.5 jit_solution(8036823648084283559)
XLA Ops:
  7.2 4.5 %fusion.60 = bf16[128,512]{1,0:T(8,128)(2,1)S(1)} fusion(bf16[1,512,4096]{2,1,0:T(8,128)(2,1)} %param.12, bf16[2,128,4096]{2,1,0:T(8,128)(2,1)} %param.8, s32[]{:T(128)S(6)} %min.28, bf16[2,128,4096]{2,1,0:T(8,128)(2,1)} %param.10), kind=kOutput, calls=%fused_computation.94 | convolution fusion | flops 539033600 | bytes 6422532 | tf_op jit(solution)/shard_map/dot_general | solution.py:15
  16.1 3.9 %fusion.63 = bf16[128,512]{1,0:T(8,128)(2,1)S(1)} fusion(bf16[1,512,4096]{2,1,0:T(8,128)(2,1)} %param.12, bf16[128,4096]{1,0:T(8,128)(2,1)S(1)} %bitcast_select_fusion, bf16[2,128,4096]{2,1,0:T(8,128)(2,1)S(1)} %copy-done.10, s32[]{:T(128)S(6)} %min.29), kind=kOutput, calls=%fused_computation.95 | convolution fusion | flops 539033600 | bytes 6422532 | tf_op jit(solution)/shard_map/dot_general | solution.py:15
  24.5 4.1 %copy.67 = bf16[256,4096]{0,1:T(8,128)(2,1)} copy(bf16[256,4096]{1,0:T(8,128)(2,1)} %bitcast.230) | data formatting | bytes 4194304 | tf_op jit(solution)/shard_map/layout_constraint | solution.py:23
  28.5 3.9 %copy.68 = bf16[256,16,256]{2,0,1:T(8,128)(2,1)} copy(bf16[256,16,256]{0,2,1:T(8,128)(2,1)} %bitcast.221) | data formatting | bytes 4194304 | tf_op jit(solution)/shard_map/reshape | solution.py:31
  32.4 7.6 %all-to-all-start = ((bf16[16,256,256]{2,1,0:T(8,128)(2,1)}), bf16[16,256,256]{2,1,0:T(8,128)(2,1)}, u32[]{:S(2)}, u32[]{:S(2)}) async-start(bf16[16,256,256]{2,1,0:T(8,128)(2,1)} %bitcast.220), calls=%async_computation | async-start | bytes 4194304 | tf_op jit(solution)/shard_map/all_to_all | solution.py:19
  40.1 4.8 %fusion.57 = bf16[256,512]{1,0:T(8,128)(2,1)} fusion(bf16[256,4096]{1,0:T(8,128)(2,1)} %bitcast.231, bf16[1,512,4096]{2,1,0:T(8,128)(2,1)} %param.11), kind=kOutput, calls=%fused_computation.93 | convolution fusion | flops 1073872896 | bytes 6553600 | tf_op jit(solution)/shard_map/dot_general | solution.py:15
  44.9 4.2 %fusion.66 = bf16[128,512]{1,0:T(8,128)(2,1)S(1)} fusion(bf16[1,512,4096]{2,1,0:T(8,128)(2,1)} %param.12, bf16[128,4096]{1,0:T(8,128)(2,1)} %collective-permute-done.1, bf16[2,128,4096]{2,1,0:T(8,128)(2,1)S(1)} %copy-done.10, s32[]{:T(128)S(6)} %min.30), kind=kOutput, calls=%fused_computation.96 | convolution fusion | flops 539033600 | bytes 6422532 | tf_op jit(solution)/shard_map/dot_general | solution.py:15
  59.1 5.7 %convolution_add_fusion = f32[256,4096]{1,0:T(8,128)} fusion(bf16[256,512]{1,0:T(8,128)(2,1)S(1)} %copy-done.32, bf16[1,512,4096]{2,1,0:T(8,128)(2,1)} %param.12, f32[4096]{0:T(1024)} %bitcast.236), kind=kOutput, calls=%fused_computation.2 | convolution fusion | flops 1074790400 | bytes 8667136 | tf_op jit(solution)/shard_map/dot_general | solution.py:15
  66.6 2.9 %fusion.72 = bf16[128,512]{1,0:T(8,128)(2,1)S(1)} fusion(bf16[1,512,4096]{2,1,0:T(8,128)(2,1)S(1)} %copy-done.3, bf16[128,4096]{1,0:T(8,128)(2,1)} %collective-permute-done.3, bf16[2,128,4096]{2,1,0:T(8,128)(2,1)S(1)} %copy-done.10, s32[]{:T(128)S(6)} %min.32), kind=kOutput, calls=%fused_computation.98 | convolution fusion | flops 539033600 | bytes 6422532 | tf_op jit(solution)/shard_map/dot_general | solution.py:15
  83.0 22.2 %collective-permute-done.5 = bf16[128,4096]{1,0:T(8,128)(2,1)S(1)} collective-permute-done((bf16[128,4096]{1,0:T(8,128)(2,1)}, bf16[128,4096]{1,0:T(8,128)(2,1)S(1)}, u32[]{:S(2)}, u32[]{:S(2)}) %collective-permute-start.5) | collective-permute-done | bytes 1048608 | tf_op jit(solution)/shard_map/ppermute | solution.py:109
  105.2 3.7 %fusion.78 = bf16[128,512]{1,0:T(8,128)(2,1)S(1)} fusion(bf16[1,512,4096]{2,1,0:T(8,128)(2,1)} %param.12, bf16[128,4096]{1,0:T(8,128)(2,1)S(1)} %collective-permute-done.5, bf16[2,128,4096]{2,1,0:T(8,128)(2,1)S(1)} %copy-done.10, s32[]{:T(128)S(6)} %min.34), kind=kOutput, calls=%fused_computation.100 | convolution fusion | flops 539033600 | bytes 6422532 | tf_op jit(solution)/shard_map/dot_general | solution.py:15
  109.7 2.2 collective-permute-start.6
  112.1 14.5 %collective-permute-done.6 = bf16[128,4096]{1,0:T(8,128)(2,1)S(1)} collective-permute-done((bf16[128,4096]{1,0:T(8,128)(2,1)S(1)}, bf16[128,4096]{1,0:T(8,128)(2,1)S(1)}, u32[]{:S(2)}, u32[]{:S(2)}) %collective-permute-start.6) | collective-permute-done | bytes 1048608 | tf_op jit(solution)/shard_map/ppermute | solution.py:109
  139.2 3.4 %fusion.54 = (bf16[128,4096]{1,0:T(8,128)(2,1)}, bf16[128,4096]{1,0:T(8,128)(2,1)S(1)}) fusion(bf16[2,128,4096]{2,1,0:T(8,128)(2,1)S(1)} %copy-done.10, bf16[128,4096]{1,0:T(8,128)(2,1)} %copy-done.20, bf16[128,4096]{1,0:T(8,128)(2,1)S(1)} %copy-done.18, bf16[128,4096]{1,0:T(8,128)(2,1)} %copy-done.19, pred[]{:T(512)S(6)} %and.96, pred[]{:T(512)S(6)} %eq.64), kind=kLoop, calls=%fused_computation.82 | loop fusion | flops 3145728 | bytes 6291458 | tf_op jit(solution)/shard_map/convert_element_type | solution.py:87
  147.8 6.9 %all-to-all-start.1 = ((bf16[16,256,256]{2,1,0:T(8,128)(2,1)}), bf16[16,256,256]{2,1,0:T(8,128)(2,1)S(1)}, u32[]{:S(2)}, u32[]{:S(2)}) async-start(bf16[16,256,256]{2,1,0:T(8,128)(2,1)} %pad_maximum_fusion), calls=%async_computation.1 | async-start | bytes 4194304 | tf_op jit(solution)/shard_map/all_to_all | solution.py:19
  159.5 7.4 %collective-permute-done.10 = bf16[2,16,4096]{2,1,0:T(8,128)(2,1)} collective-permute-done((bf16[2,16,4096]{2,1,0:T(8,128)(2,1)}, bf16[2,16,4096]{2,1,0:T(8,128)(2,1)}, u32[]{:S(2)}, u32[]{:S(2)}) %collective-permute-start.10) | collective-permute-done | bytes 262176 | tf_op jit(solution)/shard_map/ppermute | solution.py:60
  166.9 2.2 collective-permute-done.11
  169.1 4.6 %collective-permute-done.9 = bf16[2,16,4096]{2,1,0:T(8,128)(2,1)} collective-permute-done((bf16[2,16,4096]{2,1,0:T(8,128)(2,1)S(1)}, bf16[2,16,4096]{2,1,0:T(8,128)(2,1)}, u32[]{:S(2)}, u32[]{:S(2)}) %collective-permute-start.9) | collective-permute-done | bytes 262176 | tf_op jit(solution)/shard_map/ppermute | solution.py:60
  176.6 12.1 %all-to-all-done.1 = bf16[16,256,256]{2,1,0:T(8,128)(2,1)S(1)} async-done(((bf16[16,256,256]{2,1,0:T(8,128)(2,1)}), bf16[16,256,256]{2,1,0:T(8,128)(2,1)S(1)}, u32[]{:S(2)}, u32[]{:S(2)}) %all-to-all-start.1) | async-done | bytes 2097184 | tf_op jit(solution)/shard_map/all_to_all | solution.py:19
  188.6 5.4 %all-to-all-start.2 = ((bf16[128,8,384]{2,1,0:T(8,128)(2,1)}), bf16[128,8,384]{2,1,0:T(8,128)(2,1)S(1)}, u32[]{:S(2)}, u32[]{:S(2)}) async-start(bf16[128,8,384]{2,1,0:T(8,128)(2,1)} %maximum_bitcast_fusion), calls=%async_computation.2 | async-start | bytes 1572864 | tf_op jit(solution)/shard_map/all_to_all | solution.py:19
  194.0 4.4 %convolution_bitcast_fusion = f32[1,512,256]{2,1,0:T(8,128)} fusion(bf16[16,256,512]{2,1,0:T(8,128)(2,1)} %bitcast.239, bf16[16,256,256]{2,1,0:T(8,128)(2,1)S(1)} %all-to-all-done.1), kind=kOutput, calls=%fused_computation.91 | convolution fusion | flops 1073741824 | bytes 6815744 | tf_op jit(solution)/shard_map/dot_general | solution.py:15
  199.5 15.1 %all-gather.7.cloned.1.call-done = bf16[32,128,512]{2,1,0:T(8,128)(2,1)} async-done(((bf16[2,128,512]{2,1,0:T(8,128)(2,1)}), bf16[32,128,512]{2,1,0:T(8,128)(2,1)}) %all-gather.7.cloned.1.call-update) | async-done | bytes 4194320 | tf_op jit(solution)/shard_map/all_gather | solution.py:144
  214.5 4.9 %convolution_bitcast_fusion.1 = f32[512,256]{1,0:T(8,128)} fusion(bf16[16,2,128,512]{3,2,1,0:T(8,128)(2,1)} %bitcast.219, bf16[16,2,128,256]{3,2,1,0:T(8,128)(2,1)} %bitcast.43), kind=kOutput, calls=%fused_computation.92 | convolution fusion | flops 1073741824 | bytes 6815744 | tf_op jit(solution)/shard_map/dot_general | solution.py:15
  219.8 2.9 %fusion = f32[2048,256]{1,0:T(8,128)} fusion(s32[1024]{0:T(1024)S(1)} %convert_reduce_fusion.2, bf16[1024,384]{1,0:T(8,128)(2,1)S(1)} %bitcast.229), kind=kOutput, calls=%fused_computation.1 | convolution fusion | flops 1075838976 | bytes 2625536 | tf_op jit(solution)/shard_map/dot_general | solution.py:15
  (161 shorter events, 61.4 us)
Async XLA Ops:
  7.2 71.6 %copy-start = (s32[128,2,16,1]{0,3,2,1:T(1,128)S(1)}, s32[128,2,16,1]{0,3,2,1:T(1,128)}, u32[]{:S(2)}) copy-start(s32[128,2,16,1]{0,3,2,1:T(1,128)} %param.14) | copy-start | bytes 49156
  12.6 1.8 collective-permute-start
  21.8 23.2 %collective-permute-start.1 = (bf16[128,4096]{1,0:T(8,128)(2,1)}, bf16[128,4096]{1,0:T(8,128)(2,1)}, u32[]{:S(2)}, u32[]{:S(2)}) collective-permute-start(bf16[128,4096]{1,0:T(8,128)(2,1)} %fusion.2), channel_id=1, source_target_pairs={{96,80},{112,96},{97,81},{113,97},{98,82},{114,98},{99,83},{115,99... | collective-permute-start | bytes 3145736 | tf_op jit(solution)/shard_map/ppermute | solution.py:109
  32.4 50.6 %all-to-all-start = ((bf16[16,256,256]{2,1,0:T(8,128)(2,1)}), bf16[16,256,256]{2,1,0:T(8,128)(2,1)}, u32[]{:S(2)}, u32[]{:S(2)}) async-start(bf16[16,256,256]{2,1,0:T(8,128)(2,1)} %bitcast.220), calls=%async_computation | async-start | bytes 4194304 | tf_op jit(solution)/shard_map/all_to_all | solution.py:19
  40.1 148.5 %all-gather.5.cloned.1.call-start = ((), (), s32[]{:S(2)}) async-start(), calls=%async_computation.3 | async-start | bytes 4456448 | tf_op jit(solution)/shard_map/all_gather | solution.py:125
  51.3 2.6 %collective-permute-start.2 = (bf16[128,4096]{1,0:T(8,128)(2,1)S(1)}, bf16[128,4096]{1,0:T(8,128)(2,1)S(1)}, u32[]{:S(2)}, u32[]{:S(2)}) collective-permute-start(bf16[128,4096]{1,0:T(8,128)(2,1)S(1)} %fusion.3), channel_id=1, source_target_pairs={{80,64},{96,80},{81,65},{97,81},{82,66},{98,82},{83,67},{99,83},{8... | collective-permute-start | bytes 3145736 | tf_op jit(solution)/shard_map/ppermute | solution.py:109
  57.2 9.4 %collective-permute-start.3 = (bf16[128,4096]{1,0:T(8,128)(2,1)}, bf16[128,4096]{1,0:T(8,128)(2,1)}, u32[]{:S(2)}, u32[]{:S(2)}) collective-permute-start(bf16[128,4096]{1,0:T(8,128)(2,1)} %fusion.4), channel_id=1, source_target_pairs={{64,48},{80,64},{65,49},{81,65},{66,50},{82,66},{67,51},{83,67},{6... | collective-permute-start | bytes 3145736 | tf_op jit(solution)/shard_map/ppermute | solution.py:109
  58.8 155.7 %all-gather.7.cloned.1.call-start = ((), (), s32[]{:S(2)}) async-start(), calls=%async_computation.4 | async-start | bytes 4456448 | tf_op jit(solution)/shard_map/all_gather | solution.py:144
  59.1 6.4 %copy-start.16 = (bf16[128,4096]{1,0:T(8,128)(2,1)S(1)}, bf16[128,4096]{1,0:T(8,128)(2,1)}, u32[]{:S(2)}) copy-start(bf16[128,4096]{1,0:T(8,128)(2,1)} %copy-done.15) | copy-start | bytes 3145732
  59.1 7.5 %copy-start.3 = (bf16[1,512,4096]{2,1,0:T(8,128)(2,1)S(1)}, bf16[1,512,4096]{2,1,0:T(8,128)(2,1)}, u32[]{:S(2)}) copy-start(bf16[1,512,4096]{2,1,0:T(8,128)(2,1)} %param.12) | copy-start | bytes 12582916
  71.6 2.6 %collective-permute-start.4 = (bf16[128,4096]{1,0:T(8,128)(2,1)S(1)}, bf16[128,4096]{1,0:T(8,128)(2,1)S(1)}, u32[]{:S(2)}, u32[]{:S(2)}) collective-permute-start(bf16[128,4096]{1,0:T(8,128)(2,1)S(1)} %fusion.5), channel_id=1, source_target_pairs={{48,32},{64,48},{49,33},{65,49},{50,34},{66,50},{51,35},{67,51},{5... | collective-permute-start | bytes 3145736 | tf_op jit(solution)/shard_map/ppermute | solution.py:109
  77.4 27.7 %collective-permute-start.5 = (bf16[128,4096]{1,0:T(8,128)(2,1)}, bf16[128,4096]{1,0:T(8,128)(2,1)S(1)}, u32[]{:S(2)}, u32[]{:S(2)}) collective-permute-start(bf16[128,4096]{1,0:T(8,128)(2,1)} %fusion.6), channel_id=1, source_target_pairs={{32,16},{48,32},{33,17},{49,33},{34,18},{50,34},{35,19},{51,35},{3... | collective-permute-start | bytes 3145736 | tf_op jit(solution)/shard_map/ppermute | solution.py:109
  83.0 25.9 %copy-start.9 = (bf16[1,512,4096]{2,1,0:T(8,128)(2,1)S(1)}, bf16[1,512,4096]{2,1,0:T(8,128)(2,1)}, u32[]{:S(2)}) copy-start(bf16[1,512,4096]{2,1,0:T(8,128)(2,1)} %param.11) | copy-start | bytes 12582916
  108.9 17.7 %copy-start.4 = (bf16[1,512,4096]{2,1,0:T(8,128)(2,1)S(1)}, bf16[1,512,4096]{2,1,0:T(8,128)(2,1)}, u32[]{:S(2)}) copy-start(bf16[1,512,4096]{2,1,0:T(8,128)(2,1)} %param.12) | copy-start | bytes 12582916
  109.7 16.9 %collective-permute-start.6 = (bf16[128,4096]{1,0:T(8,128)(2,1)S(1)}, bf16[128,4096]{1,0:T(8,128)(2,1)S(1)}, u32[]{:S(2)}, u32[]{:S(2)}) collective-permute-start(bf16[128,4096]{1,0:T(8,128)(2,1)S(1)} %fusion.7), channel_id=1, source_target_pairs={{16,0},{32,16},{17,1},{33,17},{18,2},{34,18},{19,3},{35,19},{20,4}... | collective-permute-start | bytes 3145736 | tf_op jit(solution)/shard_map/ppermute | solution.py:109
  128.9 5.7 %collective-permute-start.7 = (bf16[128,4096]{1,0:T(8,128)(2,1)S(1)}, bf16[128,4096]{1,0:T(8,128)(2,1)S(1)}, u32[]{:S(2)}, u32[]{:S(2)}) collective-permute-start(bf16[128,4096]{1,0:T(8,128)(2,1)S(1)} %fusion.8), channel_id=1, source_target_pairs={{16,0},{17,1},{18,2},{19,3},{20,4},{21,5},{22,6},{23,7},{24,8},{25... | collective-permute-start | bytes 3145736 | tf_op jit(solution)/shard_map/ppermute | solution.py:109
  145.0 9.7 %collective-permute-start.8 = (bf16[2,4,16,4096]{3,2,0,1:T(8,128)(2,1)}, bf16[2,4,16,4096]{3,2,0,1:T(8,128)(2,1)}, u32[]{:S(2)}, u32[]{:S(2)}) collective-permute-start(bf16[2,4,16,4096]{3,2,0,1:T(8,128)(2,1)} %bitcast.216), channel_id=1, source_target_pairs={{0,16},{16,0},{32,48},{48,32},{64,80},{80,64},{96,112},{112,96},{1... | collective-permute-start | bytes 3145736 | tf_op jit(solution)/shard_map/ppermute | solution.py:55
  147.8 40.8 %all-to-all-start.1 = ((bf16[16,256,256]{2,1,0:T(8,128)(2,1)}), bf16[16,256,256]{2,1,0:T(8,128)(2,1)S(1)}, u32[]{:S(2)}, u32[]{:S(2)}) async-start(bf16[16,256,256]{2,1,0:T(8,128)(2,1)} %pad_maximum_fusion), calls=%async_computation.1 | async-start | bytes 4194304 | tf_op jit(solution)/shard_map/all_to_all | solution.py:19
  157.2 18.0 %copy-start.25 = (bf16[1024,512]{1,0:T(8,128)(2,1)S(1)}, bf16[1024,512]{1,0:T(8,128)(2,1)}, u32[]{:S(2)}) copy-start(bf16[1024,512]{1,0:T(8,128)(2,1)} %fusion.56) | copy-start | bytes 3145732
  158.0 8.9 %collective-permute-start.10 = (bf16[2,16,4096]{2,1,0:T(8,128)(2,1)}, bf16[2,16,4096]{2,1,0:T(8,128)(2,1)}, u32[]{:S(2)}, u32[]{:S(2)}) collective-permute-start(bf16[2,16,4096]{2,1,0:T(8,128)(2,1)} %get-tuple-element.83), channel_id=1, source_target_pairs={{0,64},{16,80},{32,96},{48,112},{64,0},{80,16},{96,32},{112,48},{1... | collective-permute-start | bytes 786440 | tf_op jit(solution)/shard_map/ppermute | solution.py:60
  158.0 11.1 %collective-permute-start.11 = (bf16[2,16,4096]{2,1,0:T(8,128)(2,1)}, bf16[2,16,4096]{2,1,0:T(8,128)(2,1)}, u32[]{:S(2)}, u32[]{:S(2)}) collective-permute-start(bf16[2,16,4096]{2,1,0:T(8,128)(2,1)} %get-tuple-element.82), channel_id=1, source_target_pairs={{0,96},{16,112},{32,0},{48,16},{64,32},{80,48},{96,64},{112,80},{1... | collective-permute-start | bytes 786440 | tf_op jit(solution)/shard_map/ppermute | solution.py:60
  159.0 14.7 %collective-permute-start.9 = (bf16[2,16,4096]{2,1,0:T(8,128)(2,1)S(1)}, bf16[2,16,4096]{2,1,0:T(8,128)(2,1)}, u32[]{:S(2)}, u32[]{:S(2)}) collective-permute-start(bf16[2,16,4096]{2,1,0:T(8,128)(2,1)S(1)} %get-tuple-element.81), channel_id=1, source_target_pairs={{0,32},{16,48},{32,64},{48,80},{64,96},{80,112},{96,0},{112,16},{1... | collective-permute-start | bytes 786440 | tf_op jit(solution)/shard_map/ppermute | solution.py:60
  159.5 16.1 %copy-start.35 = (bf16[1024,128]{1,0:T(8,128)(2,1)S(1)}, bf16[1024,128]{1,0:T(8,128)(2,1)}, u32[]{:S(2)}) copy-start(bf16[1024,128]{1,0:T(8,128)(2,1)} %pad.4) | copy-start | bytes 786436
  188.6 30.9 %all-to-all-start.2 = ((bf16[128,8,384]{2,1,0:T(8,128)(2,1)}), bf16[128,8,384]{2,1,0:T(8,128)(2,1)S(1)}, u32[]{:S(2)}, u32[]{:S(2)}) async-start(bf16[128,8,384]{2,1,0:T(8,128)(2,1)} %maximum_bitcast_fusion), calls=%async_computation.2 | async-start | bytes 1572864 | tf_op jit(solution)/shard_map/all_to_all | solution.py:19
  (32 other events, 95.2 us)
Sparse Core Ops, SparseCore 0:
  59.0 70.4 all-gather.4
  138.8 75.7 all-gather.6

commit v3 on v2

--- a/solution.py
+++ b/solution.py
@@ -93,6 +93,8 @@
         first = lax.dynamic_index_in_dim(embedded, clipped, 0, keepdims=False)
         if turn == 2:
             incoming, latent = after(incoming, latent)
+        if turn == sections:
+            incoming, early_gp = after(incoming, early_gp)
         if turn == 4:
             incoming, product = after(incoming, product)
         if turn == 6:
@@ -138,22 +140,25 @@
         if turn == sections - 1:
             early = terms_of(0, passed)
             arriving, *early = after(arriving, *early)
+            early_gp = exchange(early[1], "dp")
         if turn < turns - 1:
             incoming = arriving
     terms, columns = zip(early, terms_of(1, passed))
     all_h = lax.all_gather(jnp.stack([piece_of(held_h, k) for k in range(pieces)]), "dp", axis=0)
     summed = sum_over_section(jnp.stack(terms), sections, section_id)
-    all_gp = exchange(jnp.concatenate(columns, axis=1), "dp")
+    late, early_gp = after(columns[1], early_gp)
+    all_gp = [early_gp, exchange(late, "dp")]
 
     row_grads = in_columns(summed, features).reshape(-1, E)
     send = rows_major(dot(put, row_grads, ((1,), (0,))).astype(BF))
     send = jnp.concatenate([send, ids], axis=1).reshape(devices, CAP, -1)
-    send, all_gp, all_latent = after(send, all_gp, all_latent)
+    send, all_gp[1], all_latent = after(send, all_gp[1], all_latent)
     got = exchange(send, ("section", "dp")).reshape(devices * CAP, -1)
 
     all_in = all_in.reshape(replicas, pieces, rows, -1)
-    grad_up = dot(all_latent.reshape(replicas, -1, rank), all_gp, ((0, 1), (0, 1)))
-    grad_bias = jnp.sum(all_gp.astype(F32), axis=(0, 1))
+    all_latent = all_latent.reshape(replicas, pieces, rows, rank)
+    grad_up = sum(dot(all_latent[:, k], all_gp[k], ((0, 1), (0, 1))) for k in range(pieces))
+    grad_bias = sum(jnp.sum(gp.astype(F32), axis=(0, 1)) for gp in all_gp)
     grad_down = dot(all_h, all_in, ((0, 1, 2), (0, 1, 2)))
     got, grad_down = after(got, grad_down)
     got = rows_major(got)

time: 230 us -> 241 us (1.048)
  starting transfers between devices: 33.2 us -> 41.7 us
  matrix products: 61.5 us -> 65.4 us
    all_to_all x3 -> x4, waiting for transfers between devices: 12.1 us -> 28.7 us  [exchange(): return lax.all_to_all(pieces, axis, split_axis=0, concat_axis=0, tiled=True)]
    all_gather x1, waiting for transfers between devices: 15.1 us -> 0.01 us  [local(): lax.all_gather(jnp.stack([piece_of(held_h, k) for k in range(pieces)]), '...]
    all_to_all x3 -> x4, starting transfers between devices: 19.9 us -> 27.7 us  [exchange(): return lax.all_to_all(pieces, axis, split_axis=0, concat_axis=0, tiled=True)]
    ppermute x3, waiting for transfers between devices: 14.2 us -> 9.11 us  [sum_over_section(): lax.ppermute(block, 'section', ring((chips, 2), 0, d)).astype(F32)]
    dot_general x24 -> x25, matrix products: 61.5 us -> 65.4 us  [dot(): return lax.dot_general(a, b, (dims, ((), ())), preferred_element_type=F32)]
    ppermute x1, waiting for transfers between devices: 0.01 us -> 2.57 us  [sum_over_section(): other = lax.ppermute(other, 'section', ring((chips, 2), 1, 1))]
  transfers between devices with their start and end apart: 17 -> 18, of which waited for: 7 -> 8; matrix products, arithmetic and copies ran while one was open for 37% -> 36% of each run, Pallas kernels for 0% -> 0%
where the time goes in v3:
time: 241 us; the launch traced here: 240 us
  waiting for transfers between devices  76.7 us (32%)
  matrix products  65.4 us (27%)
  starting transfers between devices  41.7 us (17%)
  other arithmetic  22.3 us (9%)
  local copies, waits for them, and re-layouts  18.9 us (8%)
  between operations  14.9 us (6%)
    dot_general x25, matrix products, dot(): return lax.dot_general(a, b, (dims, ((), ())), preferred_element_type=F32)  65.4 us
    ppermute x8, waiting for transfers between devices, local(): arriving = lax.ppermute(passed, 'section', pairs)  36.3 us
    all_to_all x4, waiting for transfers between devices, exchange(): return lax.all_to_all(pieces, axis, split_axis=0, concat_axis=0, tiled=True)  28.7 us
    all_to_all x4, starting transfers between devices, exchange(): return lax.all_to_all(pieces, axis, split_axis=0, concat_axis=0, tiled=True)  27.7 us
    ppermute x8, starting transfers between devices, local(): arriving = lax.ppermute(passed, 'section', pairs)  12.4 us
    ppermute x3, waiting for transfers between devices, sum_over_section(): lax.ppermute(block, 'section', ring((chips, 2), 0, d)).astype(F32)  9.11 us
    reshape x3, local copies, waits for them, and re-layouts, in_columns(): return rows.reshape(rows.shape[0], devices, -1).transpose(1, 0, 2)  6.11 us
  transfers between devices with their start and end apart: 18, of which 8 were waited for; matrix products, arithmetic and copies ran while one was open for 36% of the time, Pallas kernels for 0%

profile of v3, /device:TPU:1, one launch (start us, length us, event | category | flops | bytes accessed | tf_op | source)
XLA Modules:
  0.0 239.7 jit_solution(693633331760509153)
XLA Ops:
  7.2 4.5 %fusion.66 = bf16[128,512]{1,0:T(8,128)(2,1)S(1)} fusion(bf16[1,512,4096]{2,1,0:T(8,128)(2,1)} %param.12, bf16[2,128,4096]{2,1,0:T(8,128)(2,1)} %param.8, s32[]{:T(128)S(6)} %min.28, bf16[2,128,4096]{2,1,0:T(8,128)(2,1)} %param.10), kind=kOutput, calls=%fused_computation.101 | convolution fusion | flops 539033600 | bytes 6422532 | tf_op jit(solution)/shard_map/dot_general | solution.py:15
  16.1 3.9 %fusion.69 = bf16[128,512]{1,0:T(8,128)(2,1)S(1)} fusion(bf16[1,512,4096]{2,1,0:T(8,128)(2,1)} %param.12, bf16[128,4096]{1,0:T(8,128)(2,1)S(1)} %bitcast_select_fusion, bf16[2,128,4096]{2,1,0:T(8,128)(2,1)S(1)} %copy-done.11, s32[]{:T(128)S(6)} %min.29), kind=kOutput, calls=%fused_computation.102 | convolution fusion | flops 539033600 | bytes 6422532 | tf_op jit(solution)/shard_map/dot_general | solution.py:15
  24.6 4.1 %copy.70 = bf16[256,4096]{0,1:T(8,128)(2,1)} copy(bf16[256,4096]{1,0:T(8,128)(2,1)} %bitcast.254) | data formatting | bytes 4194304 | tf_op jit(solution)/shard_map/layout_constraint | solution.py:23
  28.6 3.9 %copy.71 = bf16[256,16,256]{2,0,1:T(8,128)(2,1)} copy(bf16[256,16,256]{0,2,1:T(8,128)(2,1)} %bitcast.245) | data formatting | bytes 4194304 | tf_op jit(solution)/shard_map/reshape | solution.py:31
  32.5 7.6 %all-to-all-start = ((bf16[16,256,256]{2,1,0:T(8,128)(2,1)}), bf16[16,256,256]{2,1,0:T(8,128)(2,1)}, u32[]{:S(2)}, u32[]{:S(2)}) async-start(bf16[16,256,256]{2,1,0:T(8,128)(2,1)} %bitcast.244), calls=%async_computation | async-start | bytes 4194304 | tf_op jit(solution)/shard_map/all_to_all | solution.py:19
  40.2 4.8 %fusion.63 = bf16[256,512]{1,0:T(8,128)(2,1)} fusion(bf16[256,4096]{1,0:T(8,128)(2,1)} %bitcast.255, bf16[1,512,4096]{2,1,0:T(8,128)(2,1)} %param.11), kind=kOutput, calls=%fused_computation.100 | convolution fusion | flops 1073872896 | bytes 6553600 | tf_op jit(solution)/shard_map/dot_general | solution.py:15
  45.1 4.2 %fusion.72 = bf16[128,512]{1,0:T(8,128)(2,1)S(1)} fusion(bf16[1,512,4096]{2,1,0:T(8,128)(2,1)} %param.12, bf16[128,4096]{1,0:T(8,128)(2,1)} %collective-permute-done.1, bf16[2,128,4096]{2,1,0:T(8,128)(2,1)S(1)} %copy-done.11, s32[]{:T(128)S(6)} %min.30), kind=kOutput, calls=%fused_computation.103 | convolution fusion | flops 539033600 | bytes 6422532 | tf_op jit(solution)/shard_map/dot_general | solution.py:15
  59.0 5.6 %convolution_add_fusion = f32[256,4096]{1,0:T(8,128)} fusion(bf16[256,512]{1,0:T(8,128)(2,1)S(1)} %copy-done.33, bf16[1,512,4096]{2,1,0:T(8,128)(2,1)} %param.12, f32[4096]{0:T(1024)} %bitcast.261), kind=kOutput, calls=%fused_computation.2 | convolution fusion | flops 1074790400 | bytes 8667136 | tf_op jit(solution)/shard_map/dot_general | solution.py:15
  66.4 2.9 %fusion.78 = bf16[128,512]{1,0:T(8,128)(2,1)S(1)} fusion(bf16[1,512,4096]{2,1,0:T(8,128)(2,1)S(1)} %copy-done.3, bf16[128,4096]{1,0:T(8,128)(2,1)} %collective-permute-done.3, bf16[2,128,4096]{2,1,0:T(8,128)(2,1)S(1)} %copy-done.11, s32[]{:T(128)S(6)} %min.32), kind=kOutput, calls=%fused_computation.105 | convolution fusion | flops 539033600 | bytes 6422532 | tf_op jit(solution)/shard_map/dot_general | solution.py:15
  82.9 22.4 %collective-permute-done.5 = bf16[128,4096]{1,0:T(8,128)(2,1)S(1)} collective-permute-done((bf16[128,4096]{1,0:T(8,128)(2,1)}, bf16[128,4096]{1,0:T(8,128)(2,1)S(1)}, u32[]{:S(2)}, u32[]{:S(2)}) %collective-permute-start.5) | collective-permute-done | bytes 1048608 | tf_op jit(solution)/shard_map/ppermute | solution.py:111
  105.3 3.7 %fusion.84 = bf16[128,512]{1,0:T(8,128)(2,1)S(1)} fusion(bf16[1,512,4096]{2,1,0:T(8,128)(2,1)} %param.12, bf16[128,4096]{1,0:T(8,128)(2,1)S(1)} %collective-permute-done.5, bf16[2,128,4096]{2,1,0:T(8,128)(2,1)S(1)} %copy-done.11, s32[]{:T(128)S(6)} %min.34), kind=kOutput, calls=%fused_computation.107 | convolution fusion | flops 539033600 | bytes 6422532 | tf_op jit(solution)/shard_map/dot_general | solution.py:15
  112.8 13.9 %collective-permute-done.6 = bf16[128,4096]{1,0:T(8,128)(2,1)S(1)} collective-permute-done((bf16[128,4096]{1,0:T(8,128)(2,1)S(1)}, bf16[128,4096]{1,0:T(8,128)(2,1)S(1)}, u32[]{:S(2)}, u32[]{:S(2)}) %collective-permute-start.6) | collective-permute-done | bytes 1048608 | tf_op jit(solution)/shard_map/ppermute | solution.py:111
  135.6 6.9 %all-to-all-start.1 = ((bf16[16,128,256]{2,1,0:T(8,128)(2,1)}), bf16[16,128,256]{2,1,0:T(8,128)(2,1)S(1)}, u32[]{:S(2)}, u32[]{:S(2)}) async-start(bf16[16,128,256]{2,1,0:T(8,128)(2,1)} %bitcast.249), calls=%async_computation.1 | async-start | bytes 2097152 | tf_op jit(solution)/shard_map/all_to_all | solution.py:19
  143.2 15.3 %all-to-all-done.1 = bf16[16,128,256]{2,1,0:T(8,128)(2,1)S(1)} async-done(((bf16[16,128,256]{2,1,0:T(8,128)(2,1)}), bf16[16,128,256]{2,1,0:T(8,128)(2,1)S(1)}, u32[]{:S(2)}, u32[]{:S(2)}) %all-to-all-start.1) | async-done | bytes 1048608 | tf_op jit(solution)/shard_map/all_to_all | solution.py:19
  158.5 4.5 %fusion.90 = bf16[128,512]{1,0:T(8,128)(2,1)S(1)} fusion(bf16[1,512,4096]{2,1,0:T(8,128)(2,1)} %param.12, bf16[128,4096]{1,0:T(8,128)(2,1)} %collective-permute-done.7, bf16[2,128,4096]{2,1,0:T(8,128)(2,1)S(1)} %copy-done.11, s32[]{:T(128)S(6)} %min.36), kind=kOutput, calls=%fused_computation.109 | convolution fusion | flops 539033600 | bytes 6422532 | tf_op jit(solution)/shard_map/dot_general | solution.py:15
  163.0 3.0 %fusion.9 = bf16[128,4096]{1,0:T(8,128)(2,1)} fusion(bf16[128,512]{1,0:T(8,128)(2,1)S(1)} %fusion.90, bf16[1,512,4096]{2,1,0:T(8,128)(2,1)S(1)} %copy-done.10, bf16[128,4096]{1,0:T(8,128)(2,1)} %collective-permute-done.7), kind=kOutput, calls=%fused_computation.20 | convolution fusion | flops 538443776 | bytes 6422528 | tf_op jit(solution)/shard_map/dot_general | solution.py:15
  167.3 3.1 %fusion.54 = (bf16[128,4096]{1,0:T(8,128)(2,1)}, bf16[128,4096]{1,0:T(8,128)(2,1)S(1)}) fusion(bf16[2,128,4096]{2,1,0:T(8,128)(2,1)S(1)} %copy-done.11, bf16[128,4096]{1,0:T(8,128)(2,1)} %copy-done.20, bf16[128,4096]{1,0:T(8,128)(2,1)} %collective-permute-done.7, bf16[128,4096]{1,0:T(8,128)(2,1)S(1)} %copy-done.19, pred[]{:T(512)S(6)} %and.96, pred[]{:T(512)S(6)} %eq.64), kind=kLoop, calls=%fused_computation.81 | loop fusion | flops 3145728 | bytes 6291458 | tf_op jit(solution)/shard_map/convert_element_type | solution.py:87
  180.7 3.7 %all-to-all-start.2 = ((bf16[16,128,256]{2,1,0:T(8,128)(2,1)}), bf16[16,128,256]{2,1,0:T(8,128)(2,1)S(1)}, u32[]{:S(2)}, u32[]{:S(2)}) async-start(bf16[16,128,256]{2,1,0:T(8,128)(2,1)} %bitcast.248), calls=%async_computation.2 | async-start | bytes 2097152 | tf_op jit(solution)/shard_map/all_to_all | solution.py:19
  184.7 3.1 %collective-permute-done.10 = bf16[2,16,4096]{2,1,0:T(8,128)(2,1)} collective-permute-done((bf16[2,16,4096]{2,1,0:T(8,128)(2,1)}, bf16[2,16,4096]{2,1,0:T(8,128)(2,1)}, u32[]{:S(2)}, u32[]{:S(2)}) %collective-permute-start.10) | collective-permute-done | bytes 262176 | tf_op jit(solution)/shard_map/ppermute | solution.py:60
  187.8 6.0 %collective-permute-done.9 = bf16[2,16,4096]{2,1,0:T(8,128)(2,1)} collective-permute-done((bf16[2,16,4096]{2,1,0:T(8,128)(2,1)S(1)}, bf16[2,16,4096]{2,1,0:T(8,128)(2,1)}, u32[]{:S(2)}, u32[]{:S(2)}) %collective-permute-start.9) | collective-permute-done | bytes 262176 | tf_op jit(solution)/shard_map/ppermute | solution.py:60
  196.6 7.0 %all-to-all-done.2 = bf16[16,128,256]{2,1,0:T(8,128)(2,1)S(1)} async-done(((bf16[16,128,256]{2,1,0:T(8,128)(2,1)}), bf16[16,128,256]{2,1,0:T(8,128)(2,1)S(1)}, u32[]{:S(2)}, u32[]{:S(2)}) %all-to-all-start.2) | async-done | bytes 1048608 | tf_op jit(solution)/shard_map/all_to_all | solution.py:19
  203.6 9.5 %all-to-all-start.3 = ((bf16[128,8,384]{2,1,0:T(8,128)(2,1)}), bf16[128,8,384]{2,1,0:T(8,128)(2,1)S(1)}, u32[]{:S(2)}, u32[]{:S(2)}) async-start(bf16[128,8,384]{2,1,0:T(8,128)(2,1)} %maximum_bitcast_fusion), calls=%async_computation.3 | async-start | bytes 1572864 | tf_op jit(solution)/shard_map/all_to_all | solution.py:19
  218.3 4.9 %convolution_bitcast_fusion = f32[512,256]{1,0:T(8,128)} fusion(bf16[16,2,128,512]{3,2,1,0:T(8,128)(2,1)} %bitcast.243, bf16[16,2,128,256]{3,2,1,0:T(8,128)(2,1)} %bitcast.43), kind=kOutput, calls=%fused_computation.97 | convolution fusion | flops 1073741824 | bytes 6815744 | tf_op jit(solution)/shard_map/dot_general | solution.py:15
  223.3 6.4 %all-to-all-done.3 = bf16[128,8,384]{2,1,0:T(8,128)(2,1)S(1)} async-done(((bf16[128,8,384]{2,1,0:T(8,128)(2,1)}), bf16[128,8,384]{2,1,0:T(8,128)(2,1)S(1)}, u32[]{:S(2)}, u32[]{:S(2)}) %all-to-all-start.3) | async-done | bytes 786464 | tf_op jit(solution)/shard_map/all_to_all | solution.py:19
  (175 shorter events, 70.1 us)
Async XLA Ops:
  7.2 70.8 %copy-start = (s32[128,2,16,1]{0,3,2,1:T(1,128)S(1)}, s32[128,2,16,1]{0,3,2,1:T(1,128)}, u32[]{:S(2)}) copy-start(s32[128,2,16,1]{0,3,2,1:T(1,128)} %param.14) | copy-start | bytes 49156
  12.6 1.8 collective-permute-start
  21.8 23.2 %collective-permute-start.1 = (bf16[128,4096]{1,0:T(8,128)(2,1)}, bf16[128,4096]{1,0:T(8,128)(2,1)}, u32[]{:S(2)}, u32[]{:S(2)}) collective-permute-start(bf16[128,4096]{1,0:T(8,128)(2,1)} %fusion.2), channel_id=1, source_target_pairs={{96,80},{112,96},{97,81},{113,97},{98,82},{114,98},{99,83},{115,99... | collective-permute-start | bytes 3145736 | tf_op jit(solution)/shard_map/ppermute | solution.py:111
  32.5 50.4 %all-to-all-start = ((bf16[16,256,256]{2,1,0:T(8,128)(2,1)}), bf16[16,256,256]{2,1,0:T(8,128)(2,1)}, u32[]{:S(2)}, u32[]{:S(2)}) async-start(bf16[16,256,256]{2,1,0:T(8,128)(2,1)} %bitcast.244), calls=%async_computation | async-start | bytes 4194304 | tf_op jit(solution)/shard_map/all_to_all | solution.py:19
  40.2 163.4 %all-gather.5.cloned.1.call-start = ((), (), s32[]{:S(2)}) async-start(), calls=%async_computation.4 | async-start | bytes 4456448 | tf_op jit(solution)/shard_map/all_gather | solution.py:127
  51.4 2.6 %collective-permute-start.2 = (bf16[128,4096]{1,0:T(8,128)(2,1)S(1)}, bf16[128,4096]{1,0:T(8,128)(2,1)S(1)}, u32[]{:S(2)}, u32[]{:S(2)}) collective-permute-start(bf16[128,4096]{1,0:T(8,128)(2,1)S(1)} %fusion.3), channel_id=1, source_target_pairs={{80,64},{96,80},{81,65},{97,81},{82,66},{98,82},{83,67},{99,83},{8... | collective-permute-start | bytes 3145736 | tf_op jit(solution)/shard_map/ppermute | solution.py:111
  57.3 9.1 %collective-permute-start.3 = (bf16[128,4096]{1,0:T(8,128)(2,1)}, bf16[128,4096]{1,0:T(8,128)(2,1)}, u32[]{:S(2)}, u32[]{:S(2)}) collective-permute-start(bf16[128,4096]{1,0:T(8,128)(2,1)} %fusion.4), channel_id=1, source_target_pairs={{64,48},{80,64},{65,49},{81,65},{66,50},{82,66},{67,51},{83,67},{6... | collective-permute-start | bytes 3145736 | tf_op jit(solution)/shard_map/ppermute | solution.py:111
  59.0 7.4 %copy-start.3 = (bf16[1,512,4096]{2,1,0:T(8,128)(2,1)S(1)}, bf16[1,512,4096]{2,1,0:T(8,128)(2,1)}, u32[]{:S(2)}) copy-start(bf16[1,512,4096]{2,1,0:T(8,128)(2,1)} %param.12) | copy-start | bytes 12582916
  71.4 2.0 collective-permute-start.4
  76.6 28.7 %collective-permute-start.5 = (bf16[128,4096]{1,0:T(8,128)(2,1)}, bf16[128,4096]{1,0:T(8,128)(2,1)S(1)}, u32[]{:S(2)}, u32[]{:S(2)}) collective-permute-start(bf16[128,4096]{1,0:T(8,128)(2,1)} %fusion.6), channel_id=1, source_target_pairs={{32,16},{48,32},{33,17},{49,33},{34,18},{50,34},{35,19},{51,35},{3... | collective-permute-start | bytes 3145736 | tf_op jit(solution)/shard_map/ppermute | solution.py:111
  82.9 26.1 %copy-start.9 = (bf16[1,512,4096]{2,1,0:T(8,128)(2,1)S(1)}, bf16[1,512,4096]{2,1,0:T(8,128)(2,1)}, u32[]{:S(2)}) copy-start(bf16[1,512,4096]{2,1,0:T(8,128)(2,1)} %param.11) | copy-start | bytes 12582916
  109.1 17.7 %copy-start.4 = (bf16[1,512,4096]{2,1,0:T(8,128)(2,1)S(1)}, bf16[1,512,4096]{2,1,0:T(8,128)(2,1)}, u32[]{:S(2)}) copy-start(bf16[1,512,4096]{2,1,0:T(8,128)(2,1)} %param.12) | copy-start | bytes 12582916
  109.8 16.9 %collective-permute-start.6 = (bf16[128,4096]{1,0:T(8,128)(2,1)S(1)}, bf16[128,4096]{1,0:T(8,128)(2,1)S(1)}, u32[]{:S(2)}, u32[]{:S(2)}) collective-permute-start(bf16[128,4096]{1,0:T(8,128)(2,1)S(1)} %fusion.7), channel_id=1, source_target_pairs={{16,0},{32,16},{17,1},{33,17},{18,2},{34,18},{19,3},{35,19},{20,4}... | collective-permute-start | bytes 3145736 | tf_op jit(solution)/shard_map/ppermute | solution.py:111
  129.0 6.6 %collective-permute-start.7 = (bf16[128,4096]{1,0:T(8,128)(2,1)S(1)}, bf16[128,4096]{1,0:T(8,128)(2,1)}, u32[]{:S(2)}, u32[]{:S(2)}) collective-permute-start(bf16[128,4096]{1,0:T(8,128)(2,1)S(1)} %fusion.8), channel_id=1, source_target_pairs={{16,0},{17,1},{18,2},{19,3},{20,4},{21,5},{22,6},{23,7},{24,8},{25... | collective-permute-start | bytes 3145736 | tf_op jit(solution)/shard_map/ppermute | solution.py:111
  135.6 22.9 %all-to-all-start.1 = ((bf16[16,128,256]{2,1,0:T(8,128)(2,1)}), bf16[16,128,256]{2,1,0:T(8,128)(2,1)S(1)}, u32[]{:S(2)}, u32[]{:S(2)}) async-start(bf16[16,128,256]{2,1,0:T(8,128)(2,1)} %bitcast.249), calls=%async_computation.1 | async-start | bytes 2097152 | tf_op jit(solution)/shard_map/all_to_all | solution.py:19
  142.5 75.8 %all-gather.7.cloned.1.call-start = ((), (), s32[]{:S(2)}) async-start(), calls=%async_computation.5 | async-start | bytes 4456448 | tf_op jit(solution)/shard_map/all_gather | solution.py:147
  171.9 2.7 %collective-permute-start.8 = (bf16[2,4,16,4096]{3,2,0,1:T(8,128)(2,1)S(1)}, bf16[2,4,16,4096]{3,2,0,1:T(8,128)(2,1)S(1)}, u32[]{:S(2)}, u32[]{:S(2)}) collective-permute-start(bf16[2,4,16,4096]{3,2,0,1:T(8,128)(2,1)S(1)} %bitcast.258), channel_id=1, source_target_pairs={{0,16},{16,0},{32,48},{48,32},{64,80},{80,64},{96,112},{112,96},{1... | collective-permute-start | bytes 3145736 | tf_op jit(solution)/shard_map/ppermute | solution.py:55
  178.1 9.6 %collective-permute-start.10 = (bf16[2,16,4096]{2,1,0:T(8,128)(2,1)}, bf16[2,16,4096]{2,1,0:T(8,128)(2,1)}, u32[]{:S(2)}, u32[]{:S(2)}) collective-permute-start(bf16[2,16,4096]{2,1,0:T(8,128)(2,1)} %get-tuple-element.91), channel_id=1, source_target_pairs={{0,64},{16,80},{32,96},{48,112},{64,0},{80,16},{96,32},{112,48},{1... | collective-permute-start | bytes 786440 | tf_op jit(solution)/shard_map/ppermute | solution.py:60
  178.1 9.6 %collective-permute-start.11 = (bf16[2,16,4096]{2,1,0:T(8,128)(2,1)}, bf16[2,16,4096]{2,1,0:T(8,128)(2,1)}, u32[]{:S(2)}, u32[]{:S(2)}) collective-permute-start(bf16[2,16,4096]{2,1,0:T(8,128)(2,1)} %get-tuple-element.90), channel_id=1, source_target_pairs={{0,96},{16,112},{32,0},{48,16},{64,32},{80,48},{96,64},{112,80},{1... | collective-permute-start | bytes 786440 | tf_op jit(solution)/shard_map/ppermute | solution.py:60
  178.1 15.7 %collective-permute-start.9 = (bf16[2,16,4096]{2,1,0:T(8,128)(2,1)S(1)}, bf16[2,16,4096]{2,1,0:T(8,128)(2,1)}, u32[]{:S(2)}, u32[]{:S(2)}) collective-permute-start(bf16[2,16,4096]{2,1,0:T(8,128)(2,1)S(1)} %get-tuple-element.89), channel_id=1, source_target_pairs={{0,32},{16,48},{32,64},{48,80},{64,96},{80,112},{96,0},{112,16},{1... | collective-permute-start | bytes 786440 | tf_op jit(solution)/shard_map/ppermute | solution.py:60
  180.7 22.9 %all-to-all-start.2 = ((bf16[16,128,256]{2,1,0:T(8,128)(2,1)}), bf16[16,128,256]{2,1,0:T(8,128)(2,1)S(1)}, u32[]{:S(2)}, u32[]{:S(2)}) async-start(bf16[16,128,256]{2,1,0:T(8,128)(2,1)} %bitcast.248), calls=%async_computation.2 | async-start | bytes 2097152 | tf_op jit(solution)/shard_map/all_to_all | solution.py:19
  184.4 10.8 %copy-start.24 = (bf16[1024,512]{1,0:T(8,128)(2,1)S(1)}, bf16[1024,512]{1,0:T(8,128)(2,1)}, u32[]{:S(2)}) copy-start(bf16[1024,512]{1,0:T(8,128)(2,1)} %fusion.58) | copy-start | bytes 3145732
  184.7 11.0 %copy-start.37 = (bf16[1024,128]{1,0:T(8,128)(2,1)S(1)}, bf16[1024,128]{1,0:T(8,128)(2,1)}, u32[]{:S(2)}) copy-start(bf16[1024,128]{1,0:T(8,128)(2,1)} %pad.4) | copy-start | bytes 786436
  203.6 26.1 %all-to-all-start.3 = ((bf16[128,8,384]{2,1,0:T(8,128)(2,1)}), bf16[128,8,384]{2,1,0:T(8,128)(2,1)S(1)}, u32[]{:S(2)}, u32[]{:S(2)}) async-start(bf16[128,8,384]{2,1,0:T(8,128)(2,1)} %maximum_bitcast_fusion), calls=%async_computation.3 | async-start | bytes 1572864 | tf_op jit(solution)/shard_map/all_to_all | solution.py:19
  (38 other events, 126.1 us)
Sparse Core Ops, SparseCore 0:
  59.1 70.4 all-gather.4
  166.9 50.8 all-gather.6

commit v4 on v2

--- a/solution.py
+++ b/solution.py
@@ -91,8 +91,6 @@
         valid = (piece >= 0) & (piece < pieces)
         clipped = jnp.clip(piece, 0, pieces - 1)
         first = lax.dynamic_index_in_dim(embedded, clipped, 0, keepdims=False)
-        if turn == 2:
-            incoming, latent = after(incoming, latent)
         if turn == 4:
             incoming, product = after(incoming, product)
         if turn == 6:
@@ -100,8 +98,12 @@
         if turn == 0:
             incoming = cotangent[0]
         elif turn < pieces:
-            incoming = jnp.where(section_id == sections - 1, cotangent[turn], incoming)
-        gp = (incoming.astype(F32) * first.astype(F32)).astype(BF)
+            again, top = after(incoming, cotangent[turn])
+            g = jnp.where(section_id == sections - 1, cotangent[turn], incoming)
+            incoming = jnp.where(section_id == sections - 1, top, again)
+        if turn == 0 or turn >= pieces:
+            g = incoming
+        gp = (g.astype(F32) * first.astype(F32)).astype(BF)
         h = dot(gp, up, ((1,), (1,))).astype(BF)
         passed = (incoming.astype(F32) + dot(h, down, ((1,), (0,)))).astype(BF)
         if turn < turns - 1:
@@ -117,10 +119,10 @@
 
         if turn == 1:
             there = rows_major(after(layer_in, passed)[0])
-            latent = dot(there, down, ((1,), (1,))).astype(BF)
             all_in = rows_major(exchange(rows_major(in_columns(there, replicas)), "dp"))
         if turn == 3:
-            latent, _ = after(latent, passed)
+            there, _ = after(layer_in, passed)
+            latent = dot(there, down, ((1,), (1,))).astype(BF)
             product = (dot(latent, up, ((1,), (0,))) + bias[0]).reshape(pieces, rows, width)
             all_latent = lax.all_gather(latent, "dp", axis=0)
         if turn == 5:

time: 230 us -> 222 us (0.965)
  matrix products: 61.5 us -> 53.4 us
  starting transfers between devices: 33.2 us -> 29.9 us
  local copies, waits for them, and re-layouts: 17.6 us -> 20.1 us
    dot_general x24, matrix products: 61.5 us -> 53.4 us  [dot(): return lax.dot_general(a, b, (dims, ((), ())), preferred_element_type=F32)]
    ppermute x8, starting transfers between devices: 11.6 us -> 8.78 us  [local(): arriving = lax.ppermute(passed, 'section', pairs)]
  transfers between devices with their start and end apart: 17 -> 17, of which waited for: 7 -> 7; matrix products, arithmetic and copies ran while one was open for 37% -> 36% of each run, Pallas kernels for 0% -> 0%
where the time goes in v4:
time: 222 us; the launch traced here: 221 us
  waiting for transfers between devices  79 us (36%)
  matrix products  53.4 us (24%)
  starting transfers between devices  29.9 us (13%)
  other arithmetic  23.7 us (11%)
  local copies, waits for them, and re-layouts  20.1 us (9%)
  between operations  14.9 us (7%)
    dot_general x24, matrix products, dot(): return lax.dot_general(a, b, (dims, ((), ())), preferred_element_type=F32)  53.4 us
    ppermute x8, waiting for transfers between devices, local(): arriving = lax.ppermute(passed, 'section', pairs)  37.6 us
    all_to_all x3, starting transfers between devices, exchange(): return lax.all_to_all(pieces, axis, split_axis=0, concat_axis=0, tiled=True)  19.3 us
    all_gather x1, waiting for transfers between devices, local(): lax.all_gather(jnp.stack([piece_of(held_h, k) for k in range(pieces)]), '...  15.1 us
    ppermute x3, waiting for transfers between devices, sum_over_section(): lax.ppermute(block, 'section', ring((chips, 2), 0, d)).astype(F32)  14.2 us
    all_to_all x3, waiting for transfers between devices, exchange(): return lax.all_to_all(pieces, axis, split_axis=0, concat_axis=0, tiled=True)  12.1 us
    ppermute x8, starting transfers between devices, local(): arriving = lax.ppermute(passed, 'section', pairs)  8.78 us
    reshape x3, local copies, waits for them, and re-layouts, in_columns(): return rows.reshape(rows.shape[0], devices, -1).transpose(1, 0, 2)  6.33 us
  transfers between devices with their start and end apart: 17, of which 7 were waited for; matrix products, arithmetic and copies ran while one was open for 36% of the time, Pallas kernels for 0%

profile of v4, /device:TPU:1, one launch (start us, length us, event | category | flops | bytes accessed | tf_op | source)
XLA Modules:
  0.0 220.9 jit_solution(16262596887194236460)
XLA Ops:
  7.2 4.5 %fusion.60 = bf16[128,512]{1,0:T(8,128)(2,1)S(1)} fusion(bf16[1,512,4096]{2,1,0:T(8,128)(2,1)} %param.12, bf16[2,128,4096]{2,1,0:T(8,128)(2,1)} %param.8, s32[]{:T(128)S(6)} %min.28, bf16[2,128,4096]{2,1,0:T(8,128)(2,1)} %param.10), kind=kOutput, calls=%fused_computation.94 | convolution fusion | flops 539033600 | bytes 6422532 | tf_op jit(solution)/shard_map/dot_general | solution.py:15
  14.3 2.9 %slice_bitcast_fusion.1 = (bf16[128,4096]{1,0:T(8,128)(2,1)}, bf16[128,4096]{1,0:T(8,128)(2,1)S(1)}) fusion(bf16[2,128,4096]{2,1,0:T(8,128)(2,1)} %param.10), kind=kLoop, calls=%fused_computation.143 | loop fusion | bytes 4194304 | tf_op jit(solution)/shard_map/squeeze | solution.py:99
  17.3 2.9 %fusion.63 = bf16[128,512]{1,0:T(8,128)(2,1)S(1)} fusion(bf16[1,512,4096]{2,1,0:T(8,128)(2,1)S(1)} %copy-done.2, bf16[2,128,4096]{2,1,0:T(8,128)(2,1)S(1)} %copy-done.11, s32[]{:T(128)S(6)} %min.29, bf16[128,4096]{1,0:T(8,128)(2,1)S(1)} %collective-permute-done, pred[]{:T(512)S(6)} %eq.58, bf16[2,128,4096]{2,1,0:T(8,128)(2,1)} %param.10), kind=kOutput, calls=%fused_computation.95 | convolution fusion | flops 539557888 | bytes 7471109 | tf_op jit(solution)/shard_map/dot_general | solution.py:15
  23.5 4.1 %copy.67 = bf16[256,4096]{0,1:T(8,128)(2,1)} copy(bf16[256,4096]{1,0:T(8,128)(2,1)} %bitcast.233) | data formatting | bytes 4194304 | tf_op jit(solution)/shard_map/layout_constraint | solution.py:23
  27.6 3.9 %copy.68 = bf16[256,16,256]{2,0,1:T(8,128)(2,1)} copy(bf16[256,16,256]{0,2,1:T(8,128)(2,1)} %bitcast.224) | data formatting | bytes 4194304 | tf_op jit(solution)/shard_map/reshape | solution.py:31
  31.5 7.6 %all-to-all-start = ((bf16[16,256,256]{2,1,0:T(8,128)(2,1)}), bf16[16,256,256]{2,1,0:T(8,128)(2,1)}, u32[]{:S(2)}, u32[]{:S(2)}) async-start(bf16[16,256,256]{2,1,0:T(8,128)(2,1)} %bitcast.223), calls=%async_computation | async-start | bytes 4194304 | tf_op jit(solution)/shard_map/all_to_all | solution.py:19
  39.2 3.9 %fusion.66 = bf16[128,512]{1,0:T(8,128)(2,1)S(1)} fusion(bf16[1,512,4096]{2,1,0:T(8,128)(2,1)} %param.12, bf16[128,4096]{1,0:T(8,128)(2,1)S(1)} %collective-permute-done.1, bf16[2,128,4096]{2,1,0:T(8,128)(2,1)S(1)} %copy-done.11, s32[]{:T(128)S(6)} %min.30), kind=kOutput, calls=%fused_computation.96 | convolution fusion | flops 539033600 | bytes 6422532 | tf_op jit(solution)/shard_map/dot_general | solution.py:15
  50.0 2.0 fusion.57
  52.2 5.7 %convolution_add_fusion = f32[256,4096]{1,0:T(8,128)} fusion(bf16[256,512]{1,0:T(8,128)(2,1)} %fusion.57, bf16[1,512,4096]{2,1,0:T(8,128)(2,1)} %param.12, f32[4096]{0:T(1024)} %bitcast.239), kind=kOutput, calls=%fused_computation.2 | convolution fusion | flops 1074790400 | bytes 8667136 | tf_op jit(solution)/shard_map/dot_general | solution.py:15
  74.0 23.2 %collective-permute-done.5 = bf16[128,4096]{1,0:T(8,128)(2,1)S(1)} collective-permute-done((bf16[128,4096]{1,0:T(8,128)(2,1)}, bf16[128,4096]{1,0:T(8,128)(2,1)S(1)}, u32[]{:S(2)}, u32[]{:S(2)}) %collective-permute-start.5) | collective-permute-done | bytes 1048608 | tf_op jit(solution)/shard_map/ppermute | solution.py:111
  97.2 3.7 %fusion.78 = bf16[128,512]{1,0:T(8,128)(2,1)S(1)} fusion(bf16[1,512,4096]{2,1,0:T(8,128)(2,1)} %param.12, bf16[128,4096]{1,0:T(8,128)(2,1)S(1)} %collective-permute-done.5, bf16[2,128,4096]{2,1,0:T(8,128)(2,1)S(1)} %copy-done.11, s32[]{:T(128)S(6)} %min.34), kind=kOutput, calls=%fused_computation.100 | convolution fusion | flops 539033600 | bytes 6422532 | tf_op jit(solution)/shard_map/dot_general | solution.py:15
  101.7 2.2 collective-permute-start.6
  104.1 14.4 %collective-permute-done.6 = bf16[128,4096]{1,0:T(8,128)(2,1)S(1)} collective-permute-done((bf16[128,4096]{1,0:T(8,128)(2,1)S(1)}, bf16[128,4096]{1,0:T(8,128)(2,1)S(1)}, u32[]{:S(2)}, u32[]{:S(2)}) %collective-permute-start.6) | collective-permute-done | bytes 1048608 | tf_op jit(solution)/shard_map/ppermute | solution.py:111
  131.1 3.4 %fusion.53 = (bf16[128,4096]{1,0:T(8,128)(2,1)}, bf16[128,4096]{1,0:T(8,128)(2,1)S(1)}) fusion(bf16[2,128,4096]{2,1,0:T(8,128)(2,1)S(1)} %copy-done.11, bf16[128,4096]{1,0:T(8,128)(2,1)} %copy-done.21, bf16[128,4096]{1,0:T(8,128)(2,1)S(1)} %copy-done.19, bf16[128,4096]{1,0:T(8,128)(2,1)} %copy-done.20, pred[]{:T(512)S(6)} %and.96, pred[]{:T(512)S(6)} %eq.65), kind=kLoop, calls=%fused_computation.79 | loop fusion | flops 3145728 | bytes 6291458 | tf_op jit(solution)/shard_map/convert_element_type | solution.py:87
  139.7 6.3 %all-to-all-start.1 = ((bf16[16,256,256]{2,1,0:T(8,128)(2,1)}), bf16[16,256,256]{2,1,0:T(8,128)(2,1)S(1)}, u32[]{:S(2)}, u32[]{:S(2)}) async-start(bf16[16,256,256]{2,1,0:T(8,128)(2,1)} %pad_maximum_fusion), calls=%async_computation.1 | async-start | bytes 4194304 | tf_op jit(solution)/shard_map/all_to_all | solution.py:19
  150.8 7.4 %collective-permute-done.10 = bf16[2,16,4096]{2,1,0:T(8,128)(2,1)} collective-permute-done((bf16[2,16,4096]{2,1,0:T(8,128)(2,1)}, bf16[2,16,4096]{2,1,0:T(8,128)(2,1)}, u32[]{:S(2)}, u32[]{:S(2)}) %collective-permute-start.10) | collective-permute-done | bytes 262176 | tf_op jit(solution)/shard_map/ppermute | solution.py:60
  158.3 2.2 collective-permute-done.11
  160.4 4.6 %collective-permute-done.9 = bf16[2,16,4096]{2,1,0:T(8,128)(2,1)} collective-permute-done((bf16[2,16,4096]{2,1,0:T(8,128)(2,1)S(1)}, bf16[2,16,4096]{2,1,0:T(8,128)(2,1)}, u32[]{:S(2)}, u32[]{:S(2)}) %collective-permute-start.9) | collective-permute-done | bytes 262176 | tf_op jit(solution)/shard_map/ppermute | solution.py:60
  167.9 12.1 %all-to-all-done.1 = bf16[16,256,256]{2,1,0:T(8,128)(2,1)S(1)} async-done(((bf16[16,256,256]{2,1,0:T(8,128)(2,1)}), bf16[16,256,256]{2,1,0:T(8,128)(2,1)S(1)}, u32[]{:S(2)}, u32[]{:S(2)}) %all-to-all-start.1) | async-done | bytes 2097184 | tf_op jit(solution)/shard_map/all_to_all | solution.py:19
  180.0 5.4 %all-to-all-start.2 = ((bf16[128,8,384]{2,1,0:T(8,128)(2,1)}), bf16[128,8,384]{2,1,0:T(8,128)(2,1)S(1)}, u32[]{:S(2)}, u32[]{:S(2)}) async-start(bf16[128,8,384]{2,1,0:T(8,128)(2,1)} %maximum_bitcast_fusion), calls=%async_computation.2 | async-start | bytes 1572864 | tf_op jit(solution)/shard_map/all_to_all | solution.py:19
  185.4 4.4 %convolution_bitcast_fusion = f32[1,512,256]{2,1,0:T(8,128)} fusion(bf16[16,256,512]{2,1,0:T(8,128)(2,1)} %bitcast.242, bf16[16,256,256]{2,1,0:T(8,128)(2,1)S(1)} %all-to-all-done.1), kind=kOutput, calls=%fused_computation.91 | convolution fusion | flops 1073741824 | bytes 6815744 | tf_op jit(solution)/shard_map/dot_general | solution.py:15
  190.8 15.1 %all-gather.7.cloned.1.call-done = bf16[32,128,512]{2,1,0:T(8,128)(2,1)} async-done(((bf16[2,128,512]{2,1,0:T(8,128)(2,1)}), bf16[32,128,512]{2,1,0:T(8,128)(2,1)}) %all-gather.7.cloned.1.call-update) | async-done | bytes 4194320 | tf_op jit(solution)/shard_map/all_gather | solution.py:146
  205.9 4.9 %convolution_bitcast_fusion.1 = f32[512,256]{1,0:T(8,128)} fusion(bf16[16,2,128,512]{3,2,1,0:T(8,128)(2,1)} %bitcast.222, bf16[16,2,128,256]{3,2,1,0:T(8,128)(2,1)} %bitcast.43), kind=kOutput, calls=%fused_computation.92 | convolution fusion | flops 1073741824 | bytes 6815744 | tf_op jit(solution)/shard_map/dot_general | solution.py:15
  211.2 2.9 %fusion = f32[2048,256]{1,0:T(8,128)} fusion(s32[1024]{0:T(1024)S(1)} %convert_reduce_fusion.2, bf16[1024,384]{1,0:T(8,128)(2,1)S(1)} %bitcast.232), kind=kOutput, calls=%fused_computation.1 | convolution fusion | flops 1075838976 | bytes 2625536 | tf_op jit(solution)/shard_map/dot_general | solution.py:15
  (157 shorter events, 56.5 us)
Async XLA Ops:
  7.2 62.6 %copy-start = (s32[128,2,16,1]{0,3,2,1:T(1,128)S(1)}, s32[128,2,16,1]{0,3,2,1:T(1,128)}, u32[]{:S(2)}) copy-start(s32[128,2,16,1]{0,3,2,1:T(1,128)} %param.14) | copy-start | bytes 49156
  13.6 3.6 %collective-permute-start = (bf16[128,4096]{1,0:T(8,128)(2,1)}, bf16[128,4096]{1,0:T(8,128)(2,1)S(1)}, u32[]{:S(2)}, u32[]{:S(2)}) collective-permute-start(bf16[128,4096]{1,0:T(8,128)(2,1)} %fusion.1), channel_id=1, source_target_pairs={{112,96},{113,97},{114,98},{115,99},{116,100},{117,101},{118,102},... | collective-permute-start | bytes 3145736 | tf_op jit(solution)/shard_map/ppermute | solution.py:111
  22.7 16.5 %collective-permute-start.1 = (bf16[128,4096]{1,0:T(8,128)(2,1)}, bf16[128,4096]{1,0:T(8,128)(2,1)S(1)}, u32[]{:S(2)}, u32[]{:S(2)}) collective-permute-start(bf16[128,4096]{1,0:T(8,128)(2,1)} %get-tuple-element.79), channel_id=1, source_target_pairs={{96,80},{112,96},{97,81},{113,97},{98,82},{114,98},{99,83},{115,99... | collective-permute-start | bytes 3145736 | tf_op jit(solution)/shard_map/ppermute | solution.py:111
  31.5 42.5 %all-to-all-start = ((bf16[16,256,256]{2,1,0:T(8,128)(2,1)}), bf16[16,256,256]{2,1,0:T(8,128)(2,1)}, u32[]{:S(2)}, u32[]{:S(2)}) async-start(bf16[16,256,256]{2,1,0:T(8,128)(2,1)} %bitcast.223), calls=%async_computation | async-start | bytes 4194304 | tf_op jit(solution)/shard_map/all_to_all | solution.py:19
  39.2 140.8 %all-gather.5.cloned.1.call-start = ((), (), s32[]{:S(2)}) async-start(), calls=%async_computation.3 | async-start | bytes 4456448 | tf_op jit(solution)/shard_map/all_gather | solution.py:127
  43.9 2.1 collective-permute-start.2
  49.2 10.5 %collective-permute-start.3 = (bf16[128,4096]{1,0:T(8,128)(2,1)}, bf16[128,4096]{1,0:T(8,128)(2,1)S(1)}, u32[]{:S(2)}, u32[]{:S(2)}) collective-permute-start(bf16[128,4096]{1,0:T(8,128)(2,1)} %fusion.3), channel_id=1, source_target_pairs={{64,48},{80,64},{65,49},{81,65},{66,50},{82,66},{67,51},{83,67},{6... | collective-permute-start | bytes 3145736 | tf_op jit(solution)/shard_map/ppermute | solution.py:111
  52.0 153.9 %all-gather.7.cloned.1.call-start = ((), (), s32[]{:S(2)}) async-start(), calls=%async_computation.4 | async-start | bytes 4456448 | tf_op jit(solution)/shard_map/all_gather | solution.py:146
  52.2 6.4 %copy-start.17 = (bf16[128,4096]{1,0:T(8,128)(2,1)S(1)}, bf16[128,4096]{1,0:T(8,128)(2,1)}, u32[]{:S(2)}) copy-start(bf16[128,4096]{1,0:T(8,128)(2,1)} %copy-done.16) | copy-start | bytes 3145732
  52.2 7.5 %copy-start.4 = (bf16[1,512,4096]{2,1,0:T(8,128)(2,1)S(1)}, bf16[1,512,4096]{2,1,0:T(8,128)(2,1)}, u32[]{:S(2)}) copy-start(bf16[1,512,4096]{2,1,0:T(8,128)(2,1)} %param.12) | copy-start | bytes 12582916
  62.6 2.6 %collective-permute-start.4 = (bf16[128,4096]{1,0:T(8,128)(2,1)S(1)}, bf16[128,4096]{1,0:T(8,128)(2,1)S(1)}, u32[]{:S(2)}, u32[]{:S(2)}) collective-permute-start(bf16[128,4096]{1,0:T(8,128)(2,1)S(1)} %fusion.4), channel_id=1, source_target_pairs={{48,32},{64,48},{49,33},{65,49},{50,34},{66,50},{51,35},{67,51},{5... | collective-permute-start | bytes 3145736 | tf_op jit(solution)/shard_map/ppermute | solution.py:111
  68.5 28.7 %collective-permute-start.5 = (bf16[128,4096]{1,0:T(8,128)(2,1)}, bf16[128,4096]{1,0:T(8,128)(2,1)S(1)}, u32[]{:S(2)}, u32[]{:S(2)}) collective-permute-start(bf16[128,4096]{1,0:T(8,128)(2,1)} %fusion.5), channel_id=1, source_target_pairs={{32,16},{48,32},{33,17},{49,33},{34,18},{50,34},{35,19},{51,35},{3... | collective-permute-start | bytes 3145736 | tf_op jit(solution)/shard_map/ppermute | solution.py:111
  74.0 26.9 %copy-start.10 = (bf16[1,512,4096]{2,1,0:T(8,128)(2,1)S(1)}, bf16[1,512,4096]{2,1,0:T(8,128)(2,1)}, u32[]{:S(2)}) copy-start(bf16[1,512,4096]{2,1,0:T(8,128)(2,1)} %param.11) | copy-start | bytes 12582916
  100.9 17.5 %copy-start.5 = (bf16[1,512,4096]{2,1,0:T(8,128)(2,1)S(1)}, bf16[1,512,4096]{2,1,0:T(8,128)(2,1)}, u32[]{:S(2)}) copy-start(bf16[1,512,4096]{2,1,0:T(8,128)(2,1)} %param.12) | copy-start | bytes 12582916
  101.7 16.8 %collective-permute-start.6 = (bf16[128,4096]{1,0:T(8,128)(2,1)S(1)}, bf16[128,4096]{1,0:T(8,128)(2,1)S(1)}, u32[]{:S(2)}, u32[]{:S(2)}) collective-permute-start(bf16[128,4096]{1,0:T(8,128)(2,1)S(1)} %fusion.6), channel_id=1, source_target_pairs={{16,0},{32,16},{17,1},{33,17},{18,2},{34,18},{19,3},{35,19},{20,4}... | collective-permute-start | bytes 3145736 | tf_op jit(solution)/shard_map/ppermute | solution.py:111
  120.8 5.7 %collective-permute-start.7 = (bf16[128,4096]{1,0:T(8,128)(2,1)S(1)}, bf16[128,4096]{1,0:T(8,128)(2,1)S(1)}, u32[]{:S(2)}, u32[]{:S(2)}) collective-permute-start(bf16[128,4096]{1,0:T(8,128)(2,1)S(1)} %fusion.7), channel_id=1, source_target_pairs={{16,0},{17,1},{18,2},{19,3},{20,4},{21,5},{22,6},{23,7},{24,8},{25... | collective-permute-start | bytes 3145736 | tf_op jit(solution)/shard_map/ppermute | solution.py:111
  136.9 9.2 %collective-permute-start.8 = (bf16[2,4,16,4096]{3,2,0,1:T(8,128)(2,1)}, bf16[2,4,16,4096]{3,2,0,1:T(8,128)(2,1)}, u32[]{:S(2)}, u32[]{:S(2)}) collective-permute-start(bf16[2,4,16,4096]{3,2,0,1:T(8,128)(2,1)} %bitcast.219), channel_id=1, source_target_pairs={{0,16},{16,0},{32,48},{48,32},{64,80},{80,64},{96,112},{112,96},{1... | collective-permute-start | bytes 3145736 | tf_op jit(solution)/shard_map/ppermute | solution.py:55
  139.7 40.3 %all-to-all-start.1 = ((bf16[16,256,256]{2,1,0:T(8,128)(2,1)}), bf16[16,256,256]{2,1,0:T(8,128)(2,1)S(1)}, u32[]{:S(2)}, u32[]{:S(2)}) async-start(bf16[16,256,256]{2,1,0:T(8,128)(2,1)} %pad_maximum_fusion), calls=%async_computation.1 | async-start | bytes 4194304 | tf_op jit(solution)/shard_map/all_to_all | solution.py:19
  148.5 18.0 %copy-start.26 = (bf16[1024,512]{1,0:T(8,128)(2,1)S(1)}, bf16[1024,512]{1,0:T(8,128)(2,1)}, u32[]{:S(2)}) copy-start(bf16[1024,512]{1,0:T(8,128)(2,1)} %fusion.56) | copy-start | bytes 3145732
  149.4 8.9 %collective-permute-start.10 = (bf16[2,16,4096]{2,1,0:T(8,128)(2,1)}, bf16[2,16,4096]{2,1,0:T(8,128)(2,1)}, u32[]{:S(2)}, u32[]{:S(2)}) collective-permute-start(bf16[2,16,4096]{2,1,0:T(8,128)(2,1)} %get-tuple-element.87), channel_id=1, source_target_pairs={{0,64},{16,80},{32,96},{48,112},{64,0},{80,16},{96,32},{112,48},{1... | collective-permute-start | bytes 786440 | tf_op jit(solution)/shard_map/ppermute | solution.py:60
  149.4 11.1 %collective-permute-start.11 = (bf16[2,16,4096]{2,1,0:T(8,128)(2,1)}, bf16[2,16,4096]{2,1,0:T(8,128)(2,1)}, u32[]{:S(2)}, u32[]{:S(2)}) collective-permute-start(bf16[2,16,4096]{2,1,0:T(8,128)(2,1)} %get-tuple-element.86), channel_id=1, source_target_pairs={{0,96},{16,112},{32,0},{48,16},{64,32},{80,48},{96,64},{112,80},{1... | collective-permute-start | bytes 786440 | tf_op jit(solution)/shard_map/ppermute | solution.py:60
  150.4 14.7 %collective-permute-start.9 = (bf16[2,16,4096]{2,1,0:T(8,128)(2,1)S(1)}, bf16[2,16,4096]{2,1,0:T(8,128)(2,1)}, u32[]{:S(2)}, u32[]{:S(2)}) collective-permute-start(bf16[2,16,4096]{2,1,0:T(8,128)(2,1)S(1)} %get-tuple-element.85), channel_id=1, source_target_pairs={{0,32},{16,48},{32,64},{48,80},{64,96},{80,112},{96,0},{112,16},{1... | collective-permute-start | bytes 786440 | tf_op jit(solution)/shard_map/ppermute | solution.py:60
  150.8 16.1 %copy-start.34 = (bf16[1024,128]{1,0:T(8,128)(2,1)S(1)}, bf16[1024,128]{1,0:T(8,128)(2,1)}, u32[]{:S(2)}) copy-start(bf16[1024,128]{1,0:T(8,128)(2,1)} %pad.4) | copy-start | bytes 786436
  180.0 30.9 %all-to-all-start.2 = ((bf16[128,8,384]{2,1,0:T(8,128)(2,1)}), bf16[128,8,384]{2,1,0:T(8,128)(2,1)S(1)}, u32[]{:S(2)}, u32[]{:S(2)}) async-start(bf16[128,8,384]{2,1,0:T(8,128)(2,1)} %maximum_bitcast_fusion), calls=%async_computation.2 | async-start | bytes 1572864 | tf_op jit(solution)/shard_map/all_to_all | solution.py:19
  (30 other events, 84.5 us)
Sparse Core Ops, SparseCore 0:
  52.1 70.7 all-gather.4
  130.7 75.1 all-gather.6

commit v5 on v4

--- a/solution.py
+++ b/solution.py
@@ -84,7 +84,7 @@
         g = piece_of(held_g, k).astype(F32)
         bottom = jnp.where(section_id == 0, passed, jnp.zeros((), BF)).astype(F32)
         term = (g * product[k] + bottom).astype(BF)
-        return term, in_columns((g * embedded[k].astype(F32)).astype(BF), replicas)
+        return term, (g * embedded[k].astype(F32)).astype(BF)
 
     for turn in range(turns):
         piece = turn - (sections - 1 - section_id)
@@ -142,10 +142,10 @@
             arriving, *early = after(arriving, *early)
         if turn < turns - 1:
             incoming = arriving
-    terms, columns = zip(early, terms_of(1, passed))
+    terms, rows_of = zip(early, terms_of(1, passed))
     all_h = lax.all_gather(jnp.stack([piece_of(held_h, k) for k in range(pieces)]), "dp", axis=0)
     summed = sum_over_section(jnp.stack(terms), sections, section_id)
-    all_gp = exchange(jnp.concatenate(columns, axis=1), "dp")
+    all_gp = exchange(in_columns(jnp.concatenate(rows_of, axis=0), replicas), "dp")
 
     row_grads = in_columns(summed, features).reshape(-1, E)
     send = rows_major(dot(put, row_grads, ((1,), (0,))).astype(BF))

time: 222 us -> 223 us (level)
    reshape x3 -> x2, local copies, waits for them, and re-layouts: 6.33 us -> 5.45 us  [in_columns(): return rows.reshape(rows.shape[0], devices, -1).transpose(1, 0, 2)]
    unnamed x76 -> x74, local copies, waits for them, and re-layouts: 4.59 us -> 4.3 us
where the time goes in v5:
time: 223 us; the launch traced here: 222 us
  waiting for transfers between devices  80.4 us (36%)
  matrix products  53.4 us (24%)
  starting transfers between devices  29.3 us (13%)
  other arithmetic  25.1 us (11%)
  local copies, waits for them, and re-layouts  18.9 us (8%)
  between operations  14.8 us (7%)
    dot_general x24, matrix products, dot(): return lax.dot_general(a, b, (dims, ((), ())), preferred_element_type=F32)  53.4 us
    ppermute x8, waiting for transfers between devices, local(): arriving = lax.ppermute(passed, 'section', pairs)  37.6 us
    all_to_all x3, starting transfers between devices, exchange(): return lax.all_to_all(pieces, axis, split_axis=0, concat_axis=0, tiled=True)  18.5 us
    all_gather x1, waiting for transfers between devices, local(): lax.all_gather(jnp.stack([piece_of(held_h, k) for k in range(pieces)]), '...  16 us
    ppermute x3, waiting for transfers between devices, sum_over_section(): lax.ppermute(block, 'section', ring((chips, 2), 0, d)).astype(F32)  14.2 us
    all_to_all x3, waiting for transfers between devices, exchange(): return lax.all_to_all(pieces, axis, split_axis=0, concat_axis=0, tiled=True)  12.6 us
    ppermute x8, starting transfers between devices, local(): arriving = lax.ppermute(passed, 'section', pairs)  9.04 us
    convert_element_type x2, other arithmetic, terms_of(): return (term, (g * embedded[k].astype(F32)).astype(BF))  5.45 us
  transfers between devices with their start and end apart: 17, of which 7 were waited for; matrix products, arithmetic and copies ran while one was open for 36% of the time, Pallas kernels for 0%

profile of v5, /device:TPU:1, one launch (start us, length us, event | category | flops | bytes accessed | tf_op | source)
XLA Modules:
  0.0 221.9 jit_solution(14549692381583860725)
XLA Ops:
  7.2 4.5 %fusion.60 = bf16[128,512]{1,0:T(8,128)(2,1)S(1)} fusion(bf16[1,512,4096]{2,1,0:T(8,128)(2,1)} %param.12, bf16[2,128,4096]{2,1,0:T(8,128)(2,1)} %param.8, s32[]{:T(128)S(6)} %min.28, bf16[2,128,4096]{2,1,0:T(8,128)(2,1)} %param.10), kind=kOutput, calls=%fused_computation.95 | convolution fusion | flops 539033600 | bytes 6422532 | tf_op jit(solution)/shard_map/dot_general | solution.py:15
  14.3 2.9 %slice_bitcast_fusion.1 = (bf16[128,4096]{1,0:T(8,128)(2,1)}, bf16[128,4096]{1,0:T(8,128)(2,1)S(1)}) fusion(bf16[2,128,4096]{2,1,0:T(8,128)(2,1)} %param.10), kind=kLoop, calls=%fused_computation.142 | loop fusion | bytes 4194304 | tf_op jit(solution)/shard_map/squeeze | solution.py:99
  17.2 2.9 %fusion.63 = bf16[128,512]{1,0:T(8,128)(2,1)S(1)} fusion(bf16[1,512,4096]{2,1,0:T(8,128)(2,1)S(1)} %copy-done.2, bf16[2,128,4096]{2,1,0:T(8,128)(2,1)S(1)} %copy-done.11, s32[]{:T(128)S(6)} %min.29, bf16[128,4096]{1,0:T(8,128)(2,1)S(1)} %collective-permute-done, pred[]{:T(512)S(6)} %eq.58, bf16[2,128,4096]{2,1,0:T(8,128)(2,1)} %param.10), kind=kOutput, calls=%fused_computation.96 | convolution fusion | flops 539557888 | bytes 7471109 | tf_op jit(solution)/shard_map/dot_general | solution.py:15
  23.5 4.1 %copy.62 = bf16[256,4096]{0,1:T(8,128)(2,1)} copy(bf16[256,4096]{1,0:T(8,128)(2,1)} %bitcast.224) | data formatting | bytes 4194304 | tf_op jit(solution)/shard_map/layout_constraint | solution.py:23
  27.6 3.9 %copy.63 = bf16[256,16,256]{2,0,1:T(8,128)(2,1)} copy(bf16[256,16,256]{0,2,1:T(8,128)(2,1)} %bitcast.219) | data formatting | bytes 4194304 | tf_op jit(solution)/shard_map/reshape | solution.py:31
  31.5 7.6 %all-to-all-start = ((bf16[16,256,256]{2,1,0:T(8,128)(2,1)}), bf16[16,256,256]{2,1,0:T(8,128)(2,1)}, u32[]{:S(2)}, u32[]{:S(2)}) async-start(bf16[16,256,256]{2,1,0:T(8,128)(2,1)} %bitcast.216), calls=%async_computation | async-start | bytes 4194304 | tf_op jit(solution)/shard_map/all_to_all | solution.py:19
  39.2 3.9 %fusion.66 = bf16[128,512]{1,0:T(8,128)(2,1)S(1)} fusion(bf16[1,512,4096]{2,1,0:T(8,128)(2,1)} %param.12, bf16[128,4096]{1,0:T(8,128)(2,1)S(1)} %collective-permute-done.1, bf16[2,128,4096]{2,1,0:T(8,128)(2,1)S(1)} %copy-done.11, s32[]{:T(128)S(6)} %min.30), kind=kOutput, calls=%fused_computation.97 | convolution fusion | flops 539033600 | bytes 6422532 | tf_op jit(solution)/shard_map/dot_general | solution.py:15
  52.3 5.7 %convolution_add_fusion = f32[256,4096]{1,0:T(8,128)} fusion(bf16[256,512]{1,0:T(8,128)(2,1)} %fusion.57, bf16[1,512,4096]{2,1,0:T(8,128)(2,1)} %param.12, f32[4096]{0:T(1024)} %bitcast.230), kind=kOutput, calls=%fused_computation.2 | convolution fusion | flops 1074790400 | bytes 8667136 | tf_op jit(solution)/shard_map/dot_general | solution.py:15
  74.1 23.2 %collective-permute-done.5 = bf16[128,4096]{1,0:T(8,128)(2,1)S(1)} collective-permute-done((bf16[128,4096]{1,0:T(8,128)(2,1)}, bf16[128,4096]{1,0:T(8,128)(2,1)S(1)}, u32[]{:S(2)}, u32[]{:S(2)}) %collective-permute-start.5) | collective-permute-done | bytes 1048608 | tf_op jit(solution)/shard_map/ppermute | solution.py:111
  97.2 3.7 %fusion.78 = bf16[128,512]{1,0:T(8,128)(2,1)S(1)} fusion(bf16[1,512,4096]{2,1,0:T(8,128)(2,1)} %param.12, bf16[128,4096]{1,0:T(8,128)(2,1)S(1)} %collective-permute-done.5, bf16[2,128,4096]{2,1,0:T(8,128)(2,1)S(1)} %copy-done.11, s32[]{:T(128)S(6)} %min.34), kind=kOutput, calls=%fused_computation.101 | convolution fusion | flops 539033600 | bytes 6422532 | tf_op jit(solution)/shard_map/dot_general | solution.py:15
  101.7 2.2 collective-permute-start.6
  104.1 14.4 %collective-permute-done.6 = bf16[128,4096]{1,0:T(8,128)(2,1)S(1)} collective-permute-done((bf16[128,4096]{1,0:T(8,128)(2,1)S(1)}, bf16[128,4096]{1,0:T(8,128)(2,1)S(1)}, u32[]{:S(2)}, u32[]{:S(2)}) %collective-permute-start.6) | collective-permute-done | bytes 1048608 | tf_op jit(solution)/shard_map/ppermute | solution.py:111
  122.6 2.1 fusion.49
  131.0 3.4 %fusion.53 = (bf16[128,4096]{1,0:T(8,128)(2,1)}, bf16[128,4096]{1,0:T(8,128)(2,1)S(1)}) fusion(bf16[2,128,4096]{2,1,0:T(8,128)(2,1)S(1)} %copy-done.11, bf16[128,4096]{1,0:T(8,128)(2,1)} %copy-done.21, bf16[128,4096]{1,0:T(8,128)(2,1)S(1)} %copy-done.19, bf16[128,4096]{1,0:T(8,128)(2,1)} %copy-done.20, pred[]{:T(512)S(6)} %and.96, pred[]{:T(512)S(6)} %eq.65), kind=kLoop, calls=%fused_computation.79 | loop fusion | flops 3145728 | bytes 6291458 | tf_op jit(solution)/shard_map/convert_element_type | solution.py:87
  140.1 6.3 %all-to-all-start.1 = ((bf16[16,256,256]{2,1,0:T(8,128)(2,1)}), bf16[16,256,256]{2,1,0:T(8,128)(2,1)S(1)}, u32[]{:S(2)}, u32[]{:S(2)}) async-start(bf16[16,256,256]{2,1,0:T(8,128)(2,1)} %bitcast.217), calls=%async_computation.1 | async-start | bytes 4194304 | tf_op jit(solution)/shard_map/all_to_all | solution.py:19
  151.2 7.4 %collective-permute-done.10 = bf16[2,16,4096]{2,1,0:T(8,128)(2,1)} collective-permute-done((bf16[2,16,4096]{2,1,0:T(8,128)(2,1)}, bf16[2,16,4096]{2,1,0:T(8,128)(2,1)}, u32[]{:S(2)}, u32[]{:S(2)}) %collective-permute-start.10) | collective-permute-done | bytes 262176 | tf_op jit(solution)/shard_map/ppermute | solution.py:60
  158.6 2.0 collective-permute-done.11
  160.6 4.8 %collective-permute-done.9 = bf16[2,16,4096]{2,1,0:T(8,128)(2,1)} collective-permute-done((bf16[2,16,4096]{2,1,0:T(8,128)(2,1)S(1)}, bf16[2,16,4096]{2,1,0:T(8,128)(2,1)}, u32[]{:S(2)}, u32[]{:S(2)}) %collective-permute-start.9) | collective-permute-done | bytes 262176 | tf_op jit(solution)/shard_map/ppermute | solution.py:60
  168.3 12.6 %all-to-all-done.1 = bf16[16,256,256]{2,1,0:T(8,128)(2,1)S(1)} async-done(((bf16[16,256,256]{2,1,0:T(8,128)(2,1)}), bf16[16,256,256]{2,1,0:T(8,128)(2,1)S(1)}, u32[]{:S(2)}, u32[]{:S(2)}) %all-to-all-start.1) | async-done | bytes 2097184 | tf_op jit(solution)/shard_map/all_to_all | solution.py:19
  180.8 4.6 %all-to-all-start.2 = ((bf16[128,8,384]{2,1,0:T(8,128)(2,1)}), bf16[128,8,384]{2,1,0:T(8,128)(2,1)S(1)}, u32[]{:S(2)}, u32[]{:S(2)}) async-start(bf16[128,8,384]{2,1,0:T(8,128)(2,1)} %maximum_bitcast_fusion), calls=%async_computation.2 | async-start | bytes 1572864 | tf_op jit(solution)/shard_map/all_to_all | solution.py:19
  185.4 4.4 %convolution_bitcast_fusion = f32[1,512,256]{2,1,0:T(8,128)} fusion(bf16[16,256,512]{2,1,0:T(8,128)(2,1)} %bitcast.233, bf16[16,256,256]{2,1,0:T(8,128)(2,1)S(1)} %all-to-all-done.1), kind=kOutput, calls=%fused_computation.92 | convolution fusion | flops 1073741824 | bytes 6815744 | tf_op jit(solution)/shard_map/dot_general | solution.py:15
  190.9 16.0 %all-gather.7.cloned.1.call-done = bf16[32,128,512]{2,1,0:T(8,128)(2,1)} async-done(((bf16[2,128,512]{2,1,0:T(8,128)(2,1)}), bf16[32,128,512]{2,1,0:T(8,128)(2,1)}) %all-gather.7.cloned.1.call-update) | async-done | bytes 4194320 | tf_op jit(solution)/shard_map/all_gather | solution.py:146
  206.9 4.9 %convolution_bitcast_fusion.1 = f32[512,256]{1,0:T(8,128)} fusion(bf16[16,2,128,512]{3,2,1,0:T(8,128)(2,1)} %bitcast.215, bf16[16,2,128,256]{3,2,1,0:T(8,128)(2,1)} %bitcast.42), kind=kOutput, calls=%fused_computation.93 | convolution fusion | flops 1073741824 | bytes 6815744 | tf_op jit(solution)/shard_map/dot_general | solution.py:15
  212.2 2.9 %fusion = f32[2048,256]{1,0:T(8,128)} fusion(s32[1024]{0:T(1024)S(1)} %convert_reduce_fusion.2, bf16[1024,384]{1,0:T(8,128)(2,1)S(1)} %bitcast.223), kind=kOutput, calls=%fused_computation.1 | convolution fusion | flops 1075838976 | bytes 2625536 | tf_op jit(solution)/shard_map/dot_general | solution.py:15
  (154 shorter events, 56.8 us)
Async XLA Ops:
  7.2 62.6 %copy-start = (s32[128,2,16,1]{0,3,2,1:T(1,128)S(1)}, s32[128,2,16,1]{0,3,2,1:T(1,128)}, u32[]{:S(2)}) copy-start(s32[128,2,16,1]{0,3,2,1:T(1,128)} %param.14) | copy-start | bytes 49156
  13.6 3.6 %collective-permute-start = (bf16[128,4096]{1,0:T(8,128)(2,1)}, bf16[128,4096]{1,0:T(8,128)(2,1)S(1)}, u32[]{:S(2)}, u32[]{:S(2)}) collective-permute-start(bf16[128,4096]{1,0:T(8,128)(2,1)} %fusion.1), channel_id=1, source_target_pairs={{112,96},{113,97},{114,98},{115,99},{116,100},{117,101},{118,102},... | collective-permute-start | bytes 3145736 | tf_op jit(solution)/shard_map/ppermute | solution.py:111
  22.7 16.5 %collective-permute-start.1 = (bf16[128,4096]{1,0:T(8,128)(2,1)}, bf16[128,4096]{1,0:T(8,128)(2,1)S(1)}, u32[]{:S(2)}, u32[]{:S(2)}) collective-permute-start(bf16[128,4096]{1,0:T(8,128)(2,1)} %get-tuple-element.79), channel_id=1, source_target_pairs={{96,80},{112,96},{97,81},{113,97},{98,82},{114,98},{99,83},{115,99... | collective-permute-start | bytes 3145736 | tf_op jit(solution)/shard_map/ppermute | solution.py:111
  31.5 42.5 %all-to-all-start = ((bf16[16,256,256]{2,1,0:T(8,128)(2,1)}), bf16[16,256,256]{2,1,0:T(8,128)(2,1)}, u32[]{:S(2)}, u32[]{:S(2)}) async-start(bf16[16,256,256]{2,1,0:T(8,128)(2,1)} %bitcast.216), calls=%async_computation | async-start | bytes 4194304 | tf_op jit(solution)/shard_map/all_to_all | solution.py:19
  39.2 141.7 %all-gather.5.cloned.1.call-start = ((), (), s32[]{:S(2)}) async-start(), calls=%async_computation.3 | async-start | bytes 4456448 | tf_op jit(solution)/shard_map/all_gather | solution.py:127
  43.9 2.1 collective-permute-start.2
  49.2 10.5 %collective-permute-start.3 = (bf16[128,4096]{1,0:T(8,128)(2,1)}, bf16[128,4096]{1,0:T(8,128)(2,1)S(1)}, u32[]{:S(2)}, u32[]{:S(2)}) collective-permute-start(bf16[128,4096]{1,0:T(8,128)(2,1)} %fusion.3), channel_id=1, source_target_pairs={{64,48},{80,64},{65,49},{81,65},{66,50},{82,66},{67,51},{83,67},{6... | collective-permute-start | bytes 3145736 | tf_op jit(solution)/shard_map/ppermute | solution.py:111
  52.0 154.9 %all-gather.7.cloned.1.call-start = ((), (), s32[]{:S(2)}) async-start(), calls=%async_computation.4 | async-start | bytes 4456448 | tf_op jit(solution)/shard_map/all_gather | solution.py:146
  52.2 6.4 %copy-start.17 = (bf16[128,4096]{1,0:T(8,128)(2,1)S(1)}, bf16[128,4096]{1,0:T(8,128)(2,1)}, u32[]{:S(2)}) copy-start(bf16[128,4096]{1,0:T(8,128)(2,1)} %copy-done.16) | copy-start | bytes 3145732
  52.2 7.5 %copy-start.4 = (bf16[1,512,4096]{2,1,0:T(8,128)(2,1)S(1)}, bf16[1,512,4096]{2,1,0:T(8,128)(2,1)}, u32[]{:S(2)}) copy-start(bf16[1,512,4096]{2,1,0:T(8,128)(2,1)} %param.12) | copy-start | bytes 12582916
  62.6 2.6 %collective-permute-start.4 = (bf16[128,4096]{1,0:T(8,128)(2,1)S(1)}, bf16[128,4096]{1,0:T(8,128)(2,1)S(1)}, u32[]{:S(2)}, u32[]{:S(2)}) collective-permute-start(bf16[128,4096]{1,0:T(8,128)(2,1)S(1)} %fusion.4), channel_id=1, source_target_pairs={{48,32},{64,48},{49,33},{65,49},{50,34},{66,50},{51,35},{67,51},{5... | collective-permute-start | bytes 3145736 | tf_op jit(solution)/shard_map/ppermute | solution.py:111
  68.5 28.7 %collective-permute-start.5 = (bf16[128,4096]{1,0:T(8,128)(2,1)}, bf16[128,4096]{1,0:T(8,128)(2,1)S(1)}, u32[]{:S(2)}, u32[]{:S(2)}) collective-permute-start(bf16[128,4096]{1,0:T(8,128)(2,1)} %fusion.5), channel_id=1, source_target_pairs={{32,16},{48,32},{33,17},{49,33},{34,18},{50,34},{35,19},{51,35},{3... | collective-permute-start | bytes 3145736 | tf_op jit(solution)/shard_map/ppermute | solution.py:111
  74.1 26.9 %copy-start.10 = (bf16[1,512,4096]{2,1,0:T(8,128)(2,1)S(1)}, bf16[1,512,4096]{2,1,0:T(8,128)(2,1)}, u32[]{:S(2)}) copy-start(bf16[1,512,4096]{2,1,0:T(8,128)(2,1)} %param.11) | copy-start | bytes 12582916
  101.0 17.5 %copy-start.5 = (bf16[1,512,4096]{2,1,0:T(8,128)(2,1)S(1)}, bf16[1,512,4096]{2,1,0:T(8,128)(2,1)}, u32[]{:S(2)}) copy-start(bf16[1,512,4096]{2,1,0:T(8,128)(2,1)} %param.12) | copy-start | bytes 12582916
  101.7 16.8 %collective-permute-start.6 = (bf16[128,4096]{1,0:T(8,128)(2,1)S(1)}, bf16[128,4096]{1,0:T(8,128)(2,1)S(1)}, u32[]{:S(2)}, u32[]{:S(2)}) collective-permute-start(bf16[128,4096]{1,0:T(8,128)(2,1)S(1)} %fusion.6), channel_id=1, source_target_pairs={{16,0},{32,16},{17,1},{33,17},{18,2},{34,18},{19,3},{35,19},{20,4}... | collective-permute-start | bytes 3145736 | tf_op jit(solution)/shard_map/ppermute | solution.py:111
  120.8 5.6 %collective-permute-start.7 = (bf16[128,4096]{1,0:T(8,128)(2,1)S(1)}, bf16[128,4096]{1,0:T(8,128)(2,1)S(1)}, u32[]{:S(2)}, u32[]{:S(2)}) collective-permute-start(bf16[128,4096]{1,0:T(8,128)(2,1)S(1)} %fusion.7), channel_id=1, source_target_pairs={{16,0},{17,1},{18,2},{19,3},{20,4},{21,5},{22,6},{23,7},{24,8},{25... | collective-permute-start | bytes 3145736 | tf_op jit(solution)/shard_map/ppermute | solution.py:111
  136.8 9.6 %collective-permute-start.8 = (bf16[2,4,16,4096]{3,2,0,1:T(8,128)(2,1)}, bf16[2,4,16,4096]{3,2,0,1:T(8,128)(2,1)}, u32[]{:S(2)}, u32[]{:S(2)}) collective-permute-start(bf16[2,4,16,4096]{3,2,0,1:T(8,128)(2,1)} %bitcast.212), channel_id=1, source_target_pairs={{0,16},{16,0},{32,48},{48,32},{64,80},{80,64},{96,112},{112,96},{1... | collective-permute-start | bytes 3145736 | tf_op jit(solution)/shard_map/ppermute | solution.py:55
  140.1 40.7 %all-to-all-start.1 = ((bf16[16,256,256]{2,1,0:T(8,128)(2,1)}), bf16[16,256,256]{2,1,0:T(8,128)(2,1)S(1)}, u32[]{:S(2)}, u32[]{:S(2)}) async-start(bf16[16,256,256]{2,1,0:T(8,128)(2,1)} %bitcast.217), calls=%async_computation.1 | async-start | bytes 4194304 | tf_op jit(solution)/shard_map/all_to_all | solution.py:19
  148.9 18.0 %copy-start.26 = (bf16[1024,512]{1,0:T(8,128)(2,1)S(1)}, bf16[1024,512]{1,0:T(8,128)(2,1)}, u32[]{:S(2)}) copy-start(bf16[1024,512]{1,0:T(8,128)(2,1)} %fusion.56) | copy-start | bytes 3145732
  149.7 8.9 %collective-permute-start.10 = (bf16[2,16,4096]{2,1,0:T(8,128)(2,1)}, bf16[2,16,4096]{2,1,0:T(8,128)(2,1)}, u32[]{:S(2)}, u32[]{:S(2)}) collective-permute-start(bf16[2,16,4096]{2,1,0:T(8,128)(2,1)} %get-tuple-element.87), channel_id=1, source_target_pairs={{0,64},{16,80},{32,96},{48,112},{64,0},{80,16},{96,32},{112,48},{1... | collective-permute-start | bytes 786440 | tf_op jit(solution)/shard_map/ppermute | solution.py:60
  149.7 10.9 %collective-permute-start.11 = (bf16[2,16,4096]{2,1,0:T(8,128)(2,1)}, bf16[2,16,4096]{2,1,0:T(8,128)(2,1)}, u32[]{:S(2)}, u32[]{:S(2)}) collective-permute-start(bf16[2,16,4096]{2,1,0:T(8,128)(2,1)} %get-tuple-element.86), channel_id=1, source_target_pairs={{0,96},{16,112},{32,0},{48,16},{64,32},{80,48},{96,64},{112,80},{1... | collective-permute-start | bytes 786440 | tf_op jit(solution)/shard_map/ppermute | solution.py:60
  150.6 14.8 %collective-permute-start.9 = (bf16[2,16,4096]{2,1,0:T(8,128)(2,1)S(1)}, bf16[2,16,4096]{2,1,0:T(8,128)(2,1)}, u32[]{:S(2)}, u32[]{:S(2)}) collective-permute-start(bf16[2,16,4096]{2,1,0:T(8,128)(2,1)S(1)} %get-tuple-element.85), channel_id=1, source_target_pairs={{0,32},{16,48},{32,64},{48,80},{64,96},{80,112},{96,0},{112,16},{1... | collective-permute-start | bytes 786440 | tf_op jit(solution)/shard_map/ppermute | solution.py:60
  151.2 16.1 %copy-start.33 = (bf16[1024,128]{1,0:T(8,128)(2,1)S(1)}, bf16[1024,128]{1,0:T(8,128)(2,1)}, u32[]{:S(2)}) copy-start(bf16[1024,128]{1,0:T(8,128)(2,1)} %pad.4) | copy-start | bytes 786436
  180.8 31.0 %all-to-all-start.2 = ((bf16[128,8,384]{2,1,0:T(8,128)(2,1)}), bf16[128,8,384]{2,1,0:T(8,128)(2,1)S(1)}, u32[]{:S(2)}, u32[]{:S(2)}) async-start(bf16[128,8,384]{2,1,0:T(8,128)(2,1)} %maximum_bitcast_fusion), calls=%async_computation.2 | async-start | bytes 1572864 | tf_op jit(solution)/shard_map/all_to_all | solution.py:19
  (29 other events, 81.2 us)
Sparse Core Ops, SparseCore 0:
  52.1 70.7 all-gather.4
  130.6 76.2 all-gather.6
